TPU v7x, 512 devices: a whole 4x8x8 slice. The times are simulated.
512 devices in a mesh: seq: 64 (over y, z_lo, core), tp: 8 (over z_hi, x).
Axes of the slice: x: 4, y: 8, z: 8 (z_hi: 2, z_lo: 4; z = z_hi * 4 + z_lo), core: 2. Of those that a mesh axis runs over, the one named last changes fastest.
Arguments:
- frames_in: bfloat16 [16384, 1024], P('seq'), may hold values from -6 to 6
- stretch_map: int32 [64, 64], replicated, may hold values from 0 to 63, as said below
- rec_lengths: int32 [8], replicated, may hold values from 1 to 4096, 16384 in all
- windows: int32 [8], replicated, may hold values from 32 to 128
- ln1_gain: float32 [1024], replicated, may hold values from 0.6 to 5.5
- wqkv: bfloat16 [3, 1024, 1024], P(None, None, 'tp'), may hold values from -0.1875 to 0.1875
- wo: bfloat16 [1024, 1024], P('tp'), may hold values from -0.1875 to 0.1875
- ln2_gain: float32 [1024], replicated, may hold values from 0.5 to 1.5
- w1: bfloat16 [2, 1024, 1024], P(None, None, 'tp'), may hold values from -0.1875 to 0.1875
- dw_kernel: float32 [9, 1024], P(None, 'tp'), may hold values from -6 to 6
- bn_scale: float32 [1024], P('tp'), may hold values from 0.5 to 2
- bn_shift: float32 [1024], P('tp'), may hold values from -3 to 3
- w2: bfloat16 [1024, 1024], P('tp'), may hold values from -0.1875 to 0.1875
Outputs:
- block_out: bfloat16 [16384, 1024], P('seq', 'tp')
Inputs may be any that keep to these rules, and one draw needn't show every extreme that they name: Every column of stretch_map holds each of 0 to 63 exactly once. `rec_lengths`: the lengths sum to 16384.
All inputs are finite; a program needn't handle non-finite values.
Results may differ from a plain program's by a relative error of at most 0.023.
The roundings to bfloat16 on the way count: a program that leaves them out, or rounds other values in their place, can miss the bound.
Values may be sent and summed in bfloat16 or wider, within the bound.
A program may use at most 64 MiB of HBM per device.

v0:
```python
import math

import jax
import jax.numpy as jnp
from jax import lax
from jax.sharding import PartitionSpec as P

H = 8
WMAX = 128
KERNEL = 9


def extended(block, sides, width):
    for axis, dim in sides:
        count = lax.axis_size(axis)
        forward = [(i, i + 1) for i in range(count - 1)]
        backward = [(target, source) for source, target in forward]
        low = lax.ppermute(
            lax.slice_in_dim(block, block.shape[dim] - width, None, axis=dim), axis, forward
        )
        high = lax.ppermute(lax.slice_in_dim(block, 0, width, axis=dim), axis, backward)
        block = jnp.concatenate([low, block, high], axis=dim)
    return block


def layer_norm(values, gain_vector):
    wide = values.astype(jnp.float32)
    row_mean = jnp.mean(wide, axis=-1, keepdims=True)
    centred = wide - row_mean
    row_var = jnp.mean(centred * centred, axis=-1, keepdims=True)
    return centred * lax.rsqrt(row_var + 1e-05) * gain_vector


def recording_ids(positions, rec_ends):
    return jnp.sum((positions[:, None] >= rec_ends[None, :]).astype(jnp.int32), axis=1)


def allowed_pairs(query_pos, key_pos, rec_ends, windows, total):
    query_rec = recording_ids(query_pos, rec_ends)
    key_rec = recording_ids(key_pos, rec_ends)
    hits = query_rec[:, None] == jnp.arange(windows.shape[0], dtype=jnp.int32)[None, :]
    query_window = jnp.sum(jnp.where(hits, windows[None, :], 0), axis=1)
    inside = (key_pos >= 0) & (key_pos < total)
    same = query_rec[:, None] == key_rec[None, :]
    near = jnp.abs(query_pos[:, None] - key_pos[None, :]) <= query_window[:, None]
    return inside[None, :] & same & near


def project_rows(normed, wqkv):
    triple = jnp.einsum("fd,tdc->ftc", normed, wqkv, preferred_element_type=jnp.float32)
    return triple.astype(jnp.bfloat16).reshape(normed.shape[0], -1)


def gate_rows(normed, w1):
    both = jnp.einsum("fd,tdc->tfc", normed, w1, preferred_element_type=jnp.float32)
    return (both[0] * jax.nn.sigmoid(both[1])).astype(jnp.bfloat16)


def local(
    frames_in,
    stretch_map,
    rec_lengths,
    windows,
    ln1_gain,
    wqkv,
    wo,
    ln2_gain,
    w1,
    dw_kernel,
    bn_scale,
    bn_shift,
    w2,
):
    frames_dev = frames_in.shape[0]
    width = frames_in.shape[1]
    local_width = wo.shape[0]
    head_size = width // H
    shard_count = lax.axis_size("seq")
    piece_rows = frames_dev // shard_count
    seq_index = lax.axis_index("seq")
    tp_index = lax.axis_index("tp")
    column = lax.dynamic_index_in_dim(stretch_map, seq_index, axis=1, keepdims=False)
    inverse = (
        jnp.zeros((shard_count,), jnp.int32)
        .at[column]
        .set(jnp.arange(shard_count, dtype=jnp.int32))
    )
    received = lax.all_to_all(
        frames_in.reshape(shard_count, piece_rows, width),
        "seq",
        split_axis=0,
        concat_axis=0,
        tiled=True,
    )
    ordered = jnp.take(received, inverse, axis=0).reshape(frames_dev, -1)
    normed = layer_norm(ordered, ln1_gain).astype(jnp.bfloat16)
    projected = project_rows(normed, wqkv)
    own_cols = lax.dynamic_slice_in_dim(ordered, tp_index * local_width, local_width, 1)
    queries = projected[:, :local_width]
    key_value = projected[:, local_width:]
    window_rows = extended(key_value, (("seq", 0),), WMAX)
    rec_ends = jnp.cumsum(rec_lengths)
    total_frames = frames_dev * shard_count
    base = seq_index * frames_dev
    query_pos = base + jnp.arange(frames_dev, dtype=jnp.int32)
    tile_rows = min(512, frames_dev)
    tile_span = tile_rows + 2 * WMAX
    tile_count = frames_dev // tile_rows
    scale = 1.0 / math.sqrt(head_size)

    def attend_tile(tile):
        start = tile * tile_rows
        query_tile = queries.reshape(tile_rows, -1, head_size)
        key_tile = window_rows[:, :local_width].reshape(tile_span, -1, head_size)
        value_tile = window_rows[:, local_width:].reshape(tile_span, -1, head_size)
        tile_qpos = base + start + jnp.arange(tile_rows, dtype=jnp.int32)
        tile_kpos = base + start - WMAX + jnp.arange(tile_span, dtype=jnp.int32)
        usable = allowed_pairs(tile_qpos, tile_kpos, rec_ends, windows, total_frames)
        scores = (
            jnp.einsum("qhd,khd->hqk", query_tile, key_tile, preferred_element_type=jnp.float32)
            * scale
        )
        scores = jnp.where(usable, scores, -1e30)
        row_max = jnp.max(scores, axis=-1, keepdims=True)
        exp_scores = jnp.exp(scores - row_max)
        row_total = jnp.sum(exp_scores, axis=-1, keepdims=True)
        probs = (exp_scores / row_total).astype(jnp.bfloat16)
        context_tile = jnp.einsum(
            "hqk,khd->qhd", probs, value_tile, preferred_element_type=jnp.float32
        )
        return context_tile.astype(jnp.bfloat16).reshape(tile_rows, local_width)

    context = lax.map(attend_tile, jnp.arange(tile_count, dtype=jnp.int32)).reshape(
        frames_dev, local_width
    )
    head_terms = jnp.dot(context, wo, preferred_element_type=jnp.float32)
    mixed = lax.psum_scatter(
        head_terms.astype(jnp.bfloat16), "tp", scatter_dimension=1, tiled=True
    ).astype(jnp.float32)
    resid_own = (own_cols.astype(jnp.float32) + mixed).astype(jnp.bfloat16)
    resid_rows = lax.all_gather(resid_own, "tp", axis=1, tiled=True)
    normed_two = layer_norm(resid_rows, ln2_gain).astype(jnp.bfloat16)
    rim = (KERNEL - 1) // 2
    glu_rows = gate_rows(normed_two, w1)
    glu_ext = extended(glu_rows, (("seq", 0),), rim)
    own_rec = recording_ids(query_pos, rec_ends)
    running = jnp.zeros((frames_dev, local_width), jnp.float32)
    for offset in range(KERNEL):
        neighbour = query_pos + offset - rim
        valid_tap = (
            (neighbour >= 0)
            & (neighbour < total_frames)
            & (recording_ids(neighbour, rec_ends) == own_rec)
        )
        running = running + jnp.where(
            valid_tap[:, None],
            glu_ext[offset : offset + frames_dev].astype(jnp.float32) * dw_kernel[offset],
            0.0,
        )
    shifted = running * bn_scale + bn_shift
    activated = (shifted * jax.nn.sigmoid(shifted)).astype(jnp.bfloat16)
    channel_terms = jnp.dot(activated, w2, preferred_element_type=jnp.float32)
    conv_sum = lax.psum_scatter(
        channel_terms.astype(jnp.bfloat16), "tp", scatter_dimension=1, tiled=True
    ).astype(jnp.float32)
    return (resid_own.astype(jnp.float32) + conv_sum).astype(jnp.bfloat16)


def solution(mesh):
    placed = (
        P("seq", None),
        P(),
        P(),
        P(),
        P(),
        P(None, None, "tp"),
        P("tp", None),
        P(),
        P(None, None, "tp"),
        P(None, "tp"),
        P("tp"),
        P("tp"),
        P("tp", None),
    )
    return jax.shard_map(
        local, mesh=mesh, in_specs=placed, out_specs=P("seq", "tp"), check_vma=False
    )
```

profile of v0, /device:TPU:1, one launch (start us, length us, event | category | flops | bytes accessed | tf_op | source)
XLA Modules:
  0.0 299.4 jit_solution(13282036814350761545)
XLA Ops:
  6.5 2.1 reshape.293
  8.6 14.7 %all-to-all-start = ((bf16[64,4,1024]{2,1,0:T(4,128)(2,1)}), bf16[64,4,1024]{2,1,0:T(4,128)(2,1)S(1)}, u32[]{:S(2)}, u32[]{:S(2)}) async-start(bf16[64,4,1024]{2,1,0:T(4,128)(2,1)} %reshape.293), calls=%async_computation | async-start | bytes 1048576 | tf_op jit(solution)/shard_map/all_to_all | solution.py:88
  23.4 0.2 fusion.39
  23.6 0.8 scatter_custom_fusion
  24.4 0.6 copy-done.9
  25.1 0.2 reduce-window.8
  25.3 0.1 broadcast_in_dim.173
  25.4 0.1 broadcast_in_dim.174
  25.5 0.3 copy.17
  25.8 0.1 convert_reduce_fusion.10
  26.0 0.6 copy-done.4
  26.6 0.1 select_reduce_fusion
  26.7 0.1 convert_reduce_fusion.2
  26.8 14.3 %all-to-all-done = bf16[64,4,1024]{2,1,0:T(4,128)(2,1)S(1)} async-done(((bf16[64,4,1024]{2,1,0:T(4,128)(2,1)}), bf16[64,4,1024]{2,1,0:T(4,128)(2,1)S(1)}, u32[]{:S(2)}, u32[]{:S(2)}) %all-to-all-start) | async-done | bytes 524320 | tf_op jit(solution)/shard_map/all_to_all | solution.py:88
  41.1 1.0 gather_fusion
  42.1 0.1 gather.7
  42.2 0.5 convert_reduce_fusion.1
  42.7 0.1 div.37
  42.8 0.5 fusion.8
  43.3 0.1 rsqrt.20
  43.4 0.1 broadcast_select_fusion.1
  43.6 0.6 copy-done.7
  44.1 0.5 fusion.9
  44.7 3.4 %collective-permute-start = (bf16[128,256]{0,1:T(8,128)(2,1)S(1)}, bf16[128,256]{0,1:T(8,128)(2,1)S(1)}, u32[]{:S(2)}, u32[]{:S(2)}) collective-permute-start(bf16[128,256]{0,1:T(8,128)(2,1)S(1)} %get-tuple-element.37), channel_id=1, source_target_pairs={{0,8},{8,16},{16,24},{24,32},{32,40},{40,48},{48,56},{56,64},{64,7... | collective-permute-start | bytes 196616 | tf_op jit(solution)/shard_map/ppermute | solution.py:18
  48.1 1.9 collective-permute-start.1
  50.0 3.6 %collective-permute-done.1 = bf16[128,256]{0,1:T(8,128)(2,1)S(1)} collective-permute-done((bf16[128,256]{0,1:T(8,128)(2,1)S(1)}, bf16[128,256]{0,1:T(8,128)(2,1)S(1)}, u32[]{:S(2)}, u32[]{:S(2)}) %collective-permute-start.1) | collective-permute-done | bytes 65568 | tf_op jit(solution)/shard_map/ppermute | solution.py:21
  53.7 0.4 fusion.54
  54.1 0.2 fusion.19
  54.4 0.7 copy-done.5
  55.1 0.8 convolution_convert_fusion.1
  55.8 1.0 copy.18
  56.9 0.6 copy-done.3
  57.6 88.7 %reduce-scatter.7.cloned.1.call-done = bf16[128,256]{1,0:T(8,128)(2,1)} async-done(((bf16[1024,256]{1,0:T(8,128)(2,1)}), bf16[128,256]{1,0:T(8,128)(2,1)}) %reduce-scatter.7.cloned.1.call-update) | async-done | bytes 65552
  146.3 0.9 copy.19
  147.3 38.6 %all_gather.3 = bf16[256,1024]{1,0:T(8,128)(2,1)S(1)} all-gather(bf16[256,128]{1,0:T(8,128)(2,1)S(1)} %add_convert_fusion.1), channel_id=1, replica_groups=mesh['seq'=64,'tp'=8] {'tp'}, dimensions={1}, use_global_device_ids=true | all-gather | bytes 589824 | tf_op jit(solution)/shard_map/all_gather | solution.py:141
  185.9 0.1 convert_reduce_fusion
  186.1 0.3 fusion.4
  186.4 0.4 copy-done.8
  186.8 0.4 convolution_bitcast_fusion
  187.2 7.8 %collective-permute-start.2 = (bf16[4,128]{1,0:T(4,128)(2,1)S(1)}, bf16[4,128]{1,0:T(4,128)(2,1)S(1)}, u32[]{:S(2)}, u32[]{:S(2)}) collective-permute-start(bf16[4,128]{1,0:T(4,128)(2,1)S(1)} %get-tuple-element.39), channel_id=1, source_target_pairs={{0,8},{8,16},{16,24},{24,32},{32,40},{40,48},{48,56},{56,64},{64,7... | collective-permute-start | bytes 3080 | tf_op jit(solution)/shard_map/ppermute | solution.py:18
  195.0 1.9 collective-permute-start.3
  197.0 2.9 collective-permute-done.3
  199.9 0.6 copy-done.10
  200.6 1.0 convolution_convert_fusion
  201.6 1.0 copy.20
  202.6 88.4 %reduce-scatter.9.cloned.1.call-done = bf16[128,256]{1,0:T(8,128)(2,1)} async-done(((bf16[1024,256]{1,0:T(8,128)(2,1)}), bf16[128,256]{1,0:T(8,128)(2,1)}) %reduce-scatter.9.cloned.1.call-update) | async-done | bytes 65552
  291.0 0.9 copy.21
  291.9 0.7 add_convert_fusion
  (49 shorter events, 0.5 us)
Async XLA Ops:
  6.5 179.8 %copy-start = (bf16[2,1024,128]{2,1,0:T(8,128)(2,1)S(1)}, bf16[2,1024,128]{2,1,0:T(8,128)(2,1)}, u32[]{:S(2)}) copy-start(bf16[2,1024,128]{2,1,0:T(8,128)(2,1)} %param.21) | copy-start | bytes 1572868
  8.6 14.8 %copy-start.2 = (s32[64,64]{1,0:T(8,128)S(1)}, s32[64,64]{1,0:T(8,128)}, u32[]{:S(2)}) copy-start(s32[64,64]{1,0:T(8,128)} %param.14) | copy-start | bytes 49156
  8.6 16.9 %copy-start.1 = (bf16[3,1024,128]{2,1,0:T(8,128)(2,1)S(1)}, bf16[3,1024,128]{2,1,0:T(8,128)(2,1)}, u32[]{:S(2)}) copy-start(bf16[3,1024,128]{2,1,0:T(8,128)(2,1)} %param.18) | copy-start | bytes 2359300
  8.6 32.4 %all-to-all-start = ((bf16[64,4,1024]{2,1,0:T(4,128)(2,1)}), bf16[64,4,1024]{2,1,0:T(4,128)(2,1)S(1)}, u32[]{:S(2)}, u32[]{:S(2)}) async-start(bf16[64,4,1024]{2,1,0:T(4,128)(2,1)} %reshape.293), calls=%async_computation | async-start | bytes 1048576 | tf_op jit(solution)/shard_map/all_to_all | solution.py:88
  23.4 122.9 %reduce-scatter.7.cloned.1.call-start = ((), (), s32[]{:S(2)}) async-start(), calls=%async_computation.3 | async-start | bytes 589824
  24.4 0.7 copy-start.9
  25.9 0.7 copy-start.4
  43.4 0.7 copy-start.7
  44.7 5.4 %collective-permute-start = (bf16[128,256]{0,1:T(8,128)(2,1)S(1)}, bf16[128,256]{0,1:T(8,128)(2,1)S(1)}, u32[]{:S(2)}, u32[]{:S(2)}) collective-permute-start(bf16[128,256]{0,1:T(8,128)(2,1)S(1)} %get-tuple-element.37), channel_id=1, source_target_pairs={{0,8},{8,16},{16,24},{24,32},{32,40},{40,48},{48,56},{56,64},{64,7... | collective-permute-start | bytes 196616 | tf_op jit(solution)/shard_map/ppermute | solution.py:18
  48.1 5.6 %collective-permute-start.1 = (bf16[128,256]{0,1:T(8,128)(2,1)S(1)}, bf16[128,256]{0,1:T(8,128)(2,1)S(1)}, u32[]{:S(2)}, u32[]{:S(2)}) collective-permute-start(bf16[128,256]{0,1:T(8,128)(2,1)S(1)} %get-tuple-element.38), channel_id=1, source_target_pairs={{8,0},{16,8},{24,16},{32,24},{40,32},{48,40},{56,48},{64,56},{72,6... | collective-permute-start | bytes 196616 | tf_op jit(solution)/shard_map/ppermute | solution.py:21
  54.1 1.0 copy-start.5
  56.9 0.7 copy-start.3
  56.9 234.1 %reduce-scatter.9.cloned.1.call-start = ((), (), s32[]{:S(2)}) async-start(), calls=%async_computation.4 | async-start | bytes 589824
  186.1 0.7 copy-start.8
  187.2 12.7 %copy-start.6 = (bf16[128,1024]{1,0:T(8,128)(2,1)S(1)}, bf16[128,1024]{1,0:T(8,128)(2,1)}, u32[]{:S(2)}) copy-start(bf16[128,1024]{1,0:T(8,128)(2,1)} %param.25) | copy-start | bytes 786436
  187.2 9.8 %collective-permute-start.2 = (bf16[4,128]{1,0:T(4,128)(2,1)S(1)}, bf16[4,128]{1,0:T(4,128)(2,1)S(1)}, u32[]{:S(2)}, u32[]{:S(2)}) collective-permute-start(bf16[4,128]{1,0:T(4,128)(2,1)S(1)} %get-tuple-element.39), channel_id=1, source_target_pairs={{0,8},{8,16},{16,24},{24,32},{32,40},{40,48},{48,56},{56,64},{64,7... | collective-permute-start | bytes 3080 | tf_op jit(solution)/shard_map/ppermute | solution.py:18
  195.0 4.9 %collective-permute-start.3 = (bf16[4,128]{1,0:T(4,128)(2,1)S(1)}, bf16[4,128]{1,0:T(4,128)(2,1)S(1)}, u32[]{:S(2)}, u32[]{:S(2)}) collective-permute-start(bf16[4,128]{1,0:T(4,128)(2,1)S(1)} %get-tuple-element.40), channel_id=1, source_target_pairs={{8,0},{16,8},{24,16},{32,24},{40,32},{48,40},{56,48},{64,56},{72,6... | collective-permute-start | bytes 3080 | tf_op jit(solution)/shard_map/ppermute | solution.py:21
  199.9 0.7 copy-start.10
  199.9 0.7 copy-start.11
Sparse Core Ops, SparseCore 0:
  57.0 89.2 reduce-scatter.6
  202.7 88.2 reduce-scatter.8
where the time goes:
time: 301 us; the launch traced here: 299 us
  waiting for transfers between devices  198 us (66%)
  blocking collectives  38.6 us (13%)
  starting transfers between devices  29.8 us (10%)
  between operations  13.8 us (5%)
  local copies, waits for them, and re-layouts  12.9 us (4%)
  other arithmetic  3.32 us (1%)
  matrix products  3.04 us (1%)
    unnamed x4, waiting for transfers between devices  177 us
    all_gather x1, blocking collectives, local(): resid_rows = lax.all_gather(resid_own, 'tp', axis=1, tiled=True)  38.6 us
    all_to_all x1, starting transfers between devices, local(): lax.all_to_all(frames_in.reshape(shard_count, piece_rows, width), 'seq',...  14.7 us
    all_to_all x1, waiting for transfers between devices, local(): lax.all_to_all(frames_in.reshape(shard_count, piece_rows, width), 'seq',...  14.3 us
    ppermute x2, starting transfers between devices, extended(): lax.ppermute(lax.slice_in_dim(block, block.shape[dim] - width, None, axis...  11.2 us
    unnamed x29, local copies, waits for them, and re-layouts  8.44 us
    ppermute x2, waiting for transfers between devices, extended(): lax.ppermute(lax.slice_in_dim(block, 0, width, axis=dim), axis, backward)  6.51 us
  transfers between devices with their start and end apart: 7, of which 5 were waited for; matrix products, arithmetic and copies ran while one was open for 1% of the time, Pallas kernels for 0%

commit v1 on v0

v1 whole, which is shorter than its diff:
```python
import functools
import math

import jax
import jax.numpy as jnp
from jax import lax
from jax.experimental import pallas as pl
from jax.experimental.pallas import tpu as pltpu
from jax.sharding import PartitionSpec as P

MESH = pl.DeviceIdType.MESH
BF16 = jnp.bfloat16
F32 = jnp.float32
I32 = jnp.int32

SEQ = 64
TP = 8
NX = 4
ROWS = 256
HALF = 128
D = 1024
LW = 128
PIECE = 4
MSG = 16
WMAX = 128
TAPS = 9
RIM = 4
EDGE = 16


def dot(a, b):
    return jnp.dot(a, b, preferred_element_type=F32)


def dot_nt(a, b):
    return lax.dot_general(a, b, (((1,), (1,)), ((), ())), preferred_element_type=F32)


def iota(shape, dim):
    return lax.broadcasted_iota(I32, shape, dim)


def one_hot(mask):
    return jnp.where(mask, 1.0, 0.0).astype(BF16)


def layer_norm(blocks, gain_ref):
    width = blocks[0].shape[1]
    mean = sum(jnp.sum(b, axis=1, keepdims=True) for b in blocks) * (1.0 / D)
    centred = [b - mean for b in blocks]
    var = sum(jnp.sum(c * c, axis=1, keepdims=True) for c in centred) * (1.0 / D)
    inv = lax.rsqrt(var + 1e-05)
    normed = [
        (c * inv * gain_ref[:, i * width : (i + 1) * width]).astype(BF16)
        for i, c in enumerate(centred)
    ]
    return jnp.concatenate(normed, axis=1)


def block_kernel(
    frames, smap, lens, wins, gain1, wqkv, wo, gain2, w1, taps, bn_scale, bn_shift, w2,
    out,
    xin, sbuf, rbuf, frame, wq, wkv, w1v, wof, w2c, qv, kvx, ctx, act, res, glu, gluf, rim,
    lo_ref, hi_ref, start_ref, end_ref,
    ld, own_sem, a2a_s, a2a_r, xs, xr, hs, hr, wos, wor, w2s, w2r, c1s, c1r, c2s, c2r, gs, gr,
):
    s = lax.axis_index("seq")
    t = lax.axis_index("tp")
    z = t // NX
    x = lax.rem(t, NX)
    core = lax.rem(s, 2)
    mate = s + 1 - 2 * core
    left = lax.rem(s + SEQ - 1, SEQ)
    right = lax.rem(s + 1, SEQ)
    z_peer = lax.rem(t + NX, TP)

    def x_peer(d):
        return z * NX + lax.rem(x + d, NX)

    def remote(src, dst, send, recv, seq, tp):
        return pltpu.make_async_remote_copy(
            src_ref=src, dst_ref=dst, send_sem=send, recv_sem=recv,
            device_id=(seq, tp), device_id_type=MESH,
        )

    bar = pltpu.get_barrier_semaphore()

    def greet(d, carry):
        pl.semaphore_signal(bar, inc=1, device_id=(lax.rem(s + d, SEQ), t), device_id_type=MESH)
        return carry

    for d in range(1, TP):
        pl.semaphore_signal(bar, inc=1, device_id=(s, lax.rem(t + d, TP)), device_id_type=MESH)
    lax.fori_loop(1, SEQ, greet, 0)

    parity = lax.rem(x, 2)
    quarter = 2 * parity + x // 2
    loads = []

    def load(src, dst):
        cp = pltpu.make_async_copy(src, dst, ld.at[len(loads)])
        cp.start()
        loads.append(cp)
        return cp

    ld_frames = load(frames.at[:, pl.ds(pl.multiple_of(parity * 512, 512), 512)], xin)
    ld_wo = load(wo, wof.at[pl.ds(pl.multiple_of(t * LW, LW), LW)])
    ld_qkv = [
        load(wqkv.at[1], wkv.at[:, 0:LW]),
        load(wqkv.at[2], wkv.at[:, LW : 2 * LW]),
        load(wqkv.at[0], wq),
    ]
    ld_w1 = [load(w1.at[0], w1v.at[:, 0:LW]), load(w1.at[1], w1v.at[:, LW : 2 * LW])]
    ld_w2 = load(
        w2.at[:, pl.ds(pl.multiple_of(t * LW, LW), LW)],
        w2c.at[pl.ds(pl.multiple_of(t * LW, LW), LW)],
    )

    ld_frames.wait()
    o = iota((256, 256), 0)
    i = iota((256, 256), 1)
    pack = one_hot(i == 64 * ((o >> 2) & 3) + 4 * (o >> 4) + (o & 3))
    unpack = one_hot(o == 64 * ((i >> 2) & 3) + 4 * (i >> 4) + (i & 3))
    for g in range(4):
        stack = jnp.concatenate(
            [xin[64 * g : 64 * g + 64, 128 * c : 128 * c + 128] for c in range(4)], axis=0
        )
        sbuf[256 * g : 256 * g + 256, :] = dot(pack, stack).astype(BF16)

    pl.semaphore_wait(bar, SEQ - 1 + TP - 1)

    def rows16(index):
        return pl.ds(pl.multiple_of(index * MSG, MSG), MSG)

    def deal(d, carry):
        j = lax.rem(s + d, SEQ)
        remote(sbuf.at[rows16(j)], rbuf.at[rows16(s)], a2a_s, a2a_r, j, t).start()
        return carry

    lax.fori_loop(1, SEQ, deal, 0)
    own = pltpu.make_async_copy(sbuf.at[rows16(s)], rbuf.at[rows16(s)], own_sem)
    own.start()

    def wo_rows(tp, c):
        return wof.at[pl.ds(pl.multiple_of(tp * LW + c * 64, 64), 64)]

    ld_wo.wait()
    wo_first = []
    for k, peer in enumerate([x_peer(1), x_peer(2), x_peer(3), z_peer]):
        cp = remote(wo_rows(t, core), wo_rows(t, core), wos.at[k], wor.at[k], s, peer)
        cp.start()
        wo_first.append(cp)
    w2_first = []
    for k in range(1, TP):
        peer = lax.rem(t + k, TP)
        cp = remote(
            w2.at[pl.ds(pl.multiple_of(core * 64, 64), 64), pl.ds(pl.multiple_of(peer * LW, LW), LW)],
            w2c.at[pl.ds(pl.multiple_of(t * LW + core * 64, 64), 64)],
            w2s.at[k - 1], w2r.at[k - 1], s, peer,
        )
        cp.start()
        w2_first.append(cp)

    col = dot_nt(one_hot(iota((8, SEQ), 1) == s), smap[...].astype(F32).astype(BF16))
    spread = one_hot((iota((SEQ, 256), 1) >> 2) == iota((SEQ, 256), 0))
    place = dot(col.astype(BF16), spread) * 4.0 + (iota((8, 256), 1) & 3).astype(F32)
    order = one_hot(place[0:1, :] == o.astype(F32))

    pos = s * ROWS + iota((ROWS, LW), 0)
    start = jnp.zeros((ROWS, LW), I32)
    end = jnp.full((ROWS, LW), SEQ * ROWS, I32)
    reach = jnp.zeros((ROWS, LW), I32)
    total = jnp.int32(0)
    for k in range(8):
        before = total
        total = total + lens[k]
        start = jnp.where(pos >= total, total, start)
        end = jnp.where(pos < total, jnp.minimum(end, total), end)
        reach = jnp.where((pos >= before) & (pos < total), wins[k], reach)
    start_ref[...] = start
    end_ref[...] = end
    lo_ref[...] = jnp.maximum(start, pos - reach)
    hi_ref[...] = jnp.minimum(end - 1, pos + reach)

    own.wait()
    wait_all = remote(
        sbuf.at[0 : MSG * (SEQ - 1)], rbuf.at[0 : MSG * (SEQ - 1)], a2a_s, a2a_r, right, t
    )
    wait_all.wait_recv()
    parts = [dot(unpack, rbuf[256 * g : 256 * g + 256, :]).astype(BF16) for g in range(4)]
    dealt = jnp.concatenate(
        [
            jnp.concatenate([parts[g][64 * c : 64 * c + 64] for g in range(4)], axis=0)
            for c in range(4)
        ],
        axis=1,
    )
    ordered = dot(order, dealt).astype(BF16)
    frame[2 * parity] = ordered[:, 0:256]
    frame[2 * parity + 1] = ordered[:, 256:512]

    swaps = []
    for c in range(2):
        pair = []
        for n, d in enumerate((1, 3)):
            part = frame.at[quarter, c * HALF : (c + 1) * HALF]
            cp = remote(part, part, xs.at[c, n], xr.at[c, n], s, x_peer(d))
            cp.start()
            pair.append(cp)
        swaps.append(pair)

    for cp in ld_qkv:
        cp.wait()
    halos = []
    for c in range(2):
        for cp in swaps[c]:
            cp.wait_recv()
        rows = slice(c * HALF, (c + 1) * HALF)
        z1 = layer_norm([frame[q, rows, :].astype(F32) for q in range(4)], gain1)
        kvx[WMAX + c * HALF : WMAX + (c + 1) * HALF, :] = dot(z1, wkv[...]).astype(BF16)
        src = kvx.at[WMAX + c * HALF : WMAX + (c + 1) * HALF]
        if c == 0:
            cp = remote(src, kvx.at[WMAX + ROWS : 2 * WMAX + ROWS], hs.at[0], hr.at[0], left, t)
        else:
            cp = remote(src, kvx.at[0:WMAX], hs.at[1], hr.at[1], right, t)
        cp.start()
        halos.append(cp)
        qv[rows, :] = dot(z1, wq[...]).astype(BF16)

    wo_first[3].wait_recv()
    wo_next = []
    for d in range(1, NX):
        cp = remote(
            wo_rows(z_peer, core), wo_rows(z_peer, core), wos.at[3 + d], wor.at[3 + d], s, x_peer(d)
        )
        cp.start()
        wo_next.append(cp)
    wo_swap = []

    def give_wo(tp):
        k = 7 + len(wo_swap)
        cp = remote(wo_rows(tp, core), wo_rows(tp, core), wos.at[k], wor.at[k], mate, t)
        cp.start()
        wo_swap.append(cp)

    give_wo(z_peer)
    for d in range(1, NX):
        wo_first[d - 1].wait_recv()
        give_wo(x_peer(NX - d))

    def send_group(buf, rows, send, recv):
        sent = []
        for k, peer in enumerate([z_peer, x_peer(1), x_peer(2), x_peer(3)]):
            cp = remote(buf.at[t, rows], buf.at[t, rows], send.at[k], recv.at[k], s, peer)
            cp.start()
            sent.append(cp)
        return sent

    def pass_on(buf, rows, send, recv, sent):
        sent[0].wait_recv()
        for d in range(1, NX):
            cp = remote(
                buf.at[z_peer, rows], buf.at[z_peer, rows], send.at[3 + d], recv.at[3 + d],
                s, x_peer(d),
            )
            cp.start()
            sent.append(cp)

    def whole(buf, rows, sent):
        for cp in sent[1:]:
            cp.wait_recv()
        return jnp.concatenate([buf[k, rows, :] for k in range(TP)], axis=1)

    scale = 1.0 / math.sqrt(LW)
    sent1 = {}
    for c in (1, 0):
        rows = slice(c * HALF, (c + 1) * HALF)
        keys = slice(c * HALF, c * HALF + HALF + 2 * WMAX)
        halos[1 - c].wait_recv()
        scores = dot_nt(qv[rows, :], kvx[keys, 0:LW]) * scale
        kpos = s * ROWS + c * HALF - WMAX + iota((HALF, HALF + 2 * WMAX), 1)
        low = jnp.concatenate([lo_ref[rows, :]] * 3, axis=1)
        high = jnp.concatenate([hi_ref[rows, :]] * 3, axis=1)
        scores = jnp.where((kpos >= low) & (kpos <= high), scores, -1e30)
        peak = jnp.max(scores, axis=1, keepdims=True)
        weights = jnp.exp(scores - peak)
        weights = (weights / jnp.sum(weights, axis=1, keepdims=True)).astype(BF16)
        ctx[t, rows, :] = dot(weights, kvx[keys, LW : 2 * LW]).astype(BF16)
        sent1[c] = send_group(ctx, rows, c1s.at[c], c1r.at[c])

    for d in range(1, NX):
        wo_next[d - 1].wait_recv()
        give_wo(lax.rem(x_peer(NX - d) + NX, TP))
    w2_swap = []
    for k in range(1, TP):
        w2_first[k - 1].wait_recv()
        part = w2c.at[
            pl.ds(pl.multiple_of(lax.rem(t + TP - k, TP) * LW + core * 64, 64), 64)
        ]
        cp = remote(part, part, w2s.at[6 + k], w2r.at[6 + k], mate, t)
        cp.start()
        w2_swap.append(cp)

    for c in (1, 0):
        pass_on(ctx, slice(c * HALF, (c + 1) * HALF), c1s.at[c], c1r.at[c], sent1[c])
    for cp in wo_swap:
        cp.wait_recv()
    for cp in ld_w1:
        cp.wait()

    edges = {}
    for c in (1, 0):
        rows = slice(c * HALF, (c + 1) * HALF)
        attn = dot(whole(ctx, rows, sent1[c]), wof[...])
        resid = [
            (frame[q, rows, :].astype(F32) + attn[:, 256 * q : 256 * q + 256]).astype(BF16)
            for q in range(4)
        ]
        for q in range(4):
            res[2 * q, rows, :] = resid[q][:, 0:LW]
            res[2 * q + 1, rows, :] = resid[q][:, LW : 2 * LW]
        z2 = layer_norm([r.astype(F32) for r in resid], gain2)
        both = dot(z2, w1v[...])
        gated = (both[:, 0:LW] * jax.nn.sigmoid(both[:, LW : 2 * LW])).astype(BF16)
        glu[rows, :] = gated
        gluf[EDGE + c * HALF : EDGE + (c + 1) * HALF, :] = gated.astype(F32)
        if c == 1:
            cp = remote(glu.at[ROWS - EDGE : ROWS], rim.at[0], gs.at[0], gr.at[0], right, t)
        else:
            cp = remote(glu.at[0:EDGE], rim.at[1], gs.at[1], gr.at[1], left, t)
        cp.start()
        edges[c] = cp

    sent2 = {}
    for c in (1, 0):
        rows = slice(c * HALF, (c + 1) * HALF)
        edges[1 - c].wait_recv()
        if c == 1:
            gluf[EDGE + ROWS : 2 * EDGE + ROWS, :] = rim[1].astype(F32)
        else:
            gluf[0:EDGE, :] = rim[0].astype(F32)
        at = s * ROWS + c * HALF + iota((HALF, LW), 0)
        room_low = start_ref[rows, :] - at
        room_high = end_ref[rows, :] - at
        conv = jnp.zeros((HALF, LW), F32)
        for k in range(TAPS):
            first = EDGE + c * HALF + k - RIM
            valid = (room_low <= k - RIM) & (room_high > k - RIM)
            conv = conv + jnp.where(valid, gluf[first : first + HALF, :] * taps[k : k + 1, :], 0.0)
        shifted = conv * bn_scale[...] + bn_shift[...]
        act[t, rows, :] = (shifted * jax.nn.sigmoid(shifted)).astype(BF16)
        sent2[c] = send_group(act, rows, c2s.at[c], c2r.at[c])

    ld_w2.wait()
    for cp in w2_swap:
        cp.wait_recv()
    for c in (1, 0):
        pass_on(act, slice(c * HALF, (c + 1) * HALF), c2s.at[c], c2r.at[c], sent2[c])
    for c in (1, 0):
        rows = slice(c * HALF, (c + 1) * HALF)
        summed = dot(whole(act, rows, sent2[c]), w2c[...])
        out[rows, :] = (res[t, rows, :].astype(F32) + summed).astype(BF16)

    wait_all.wait_send()
    sends = swaps[0] + swaps[1] + halos + wo_first + wo_next + wo_swap + w2_first + w2_swap
    sends += sent1[0] + sent1[1] + sent2[0] + sent2[1] + [edges[0], edges[1]]
    for cp in sends:
        cp.wait_send()


def local(
    frames_in, stretch_map, rec_lengths, windows, ln1_gain, wqkv, wo, ln2_gain, w1,
    dw_kernel, bn_scale, bn_shift, w2,
):
    vmem = pl.BlockSpec(memory_space=pltpu.VMEM)
    smem = pl.BlockSpec(memory_space=pltpu.SMEM)
    hbm = pl.BlockSpec(memory_space=pl.ANY)
    dma = pltpu.SemaphoreType.DMA
    return pl.pallas_call(
        block_kernel,
        out_shape=jax.ShapeDtypeStruct((ROWS, LW), BF16),
        in_specs=[hbm, vmem, smem, smem, vmem, hbm, hbm, vmem, hbm, vmem, vmem, vmem, hbm],
        out_specs=vmem,
        scratch_shapes=[
            pltpu.VMEM((ROWS, 512), BF16),
            pltpu.VMEM((SEQ * MSG, 128), BF16),
            pltpu.VMEM((SEQ * MSG, 128), BF16),
            pltpu.VMEM((4, ROWS, 256), BF16),
            pltpu.VMEM((D, LW), BF16),
            pltpu.VMEM((D, 2 * LW), BF16),
            pltpu.VMEM((D, 2 * LW), BF16),
            pltpu.VMEM((D, D), BF16),
            pltpu.VMEM((D, LW), BF16),
            pltpu.VMEM((ROWS, LW), BF16),
            pltpu.VMEM((ROWS + 2 * WMAX, 2 * LW), BF16),
            pltpu.VMEM((TP, ROWS, LW), BF16),
            pltpu.VMEM((TP, ROWS, LW), BF16),
            pltpu.VMEM((TP, ROWS, LW), BF16),
            pltpu.VMEM((ROWS, LW), BF16),
            pltpu.VMEM((ROWS + 2 * EDGE, LW), F32),
            pltpu.VMEM((2, EDGE, LW), BF16),
            pltpu.VMEM((ROWS, LW), I32),
            pltpu.VMEM((ROWS, LW), I32),
            pltpu.VMEM((ROWS, LW), I32),
            pltpu.VMEM((ROWS, LW), I32),
            dma((8,)),
            dma,
            dma,
            dma,
            dma((2, 2)),
            dma((2, 2)),
            dma((2,)),
            dma((2,)),
            dma((14,)),
            dma((14,)),
            dma((14,)),
            dma((14,)),
            dma((2, 7)),
            dma((2, 7)),
            dma((2, 7)),
            dma((2, 7)),
            dma((2,)),
            dma((2,)),
        ],
        compiler_params=pltpu.CompilerParams(
            collective_id=0, has_side_effects=True, vmem_limit_bytes=48 << 20
        ),
        name="encoder_block",
    )(
        frames_in, stretch_map, rec_lengths, windows, ln1_gain.reshape(1, D), wqkv, wo,
        ln2_gain.reshape(1, D), w1, dw_kernel, bn_scale.reshape(1, LW),
        bn_shift.reshape(1, LW), w2,
    )


def solution(mesh):
    placed = (
        P("seq", None),
        P(),
        P(),
        P(),
        P(),
        P(None, None, "tp"),
        P("tp", None),
        P(),
        P(None, None, "tp"),
        P(None, "tp"),
        P("tp"),
        P("tp"),
        P("tp", None),
    )
    return jax.shard_map(
        local, mesh=mesh, in_specs=placed, out_specs=P("seq", "tp"), check_vma=False
    )
```

time: 301 us -> 77.3 us (0.26)
  waiting for transfers between devices: 198 us -> 0 us
  Pallas kernels: 0 us -> 68.2 us
  blocking collectives: 38.6 us -> 0 us
  starting transfers between devices: 29.8 us -> 0 us
  between operations: 13.8 us -> 0.04 us
  local copies, waits for them, and re-layouts: 12.9 us -> 8.58 us
  other arithmetic: 3.32 us -> 0 us
  matrix products: 3.04 us -> 0 us
    unnamed x4 -> x0, waiting for transfers between devices: 177 us -> none
    pallas_call x0 -> x1, Pallas kernels: none -> 68.2 us  [local(): pl.pallas_call(block_kernel, out_shape=jax.ShapeDtypeStruct((ROWS, LW), B...]
    all_gather x1 -> x0, blocking collectives: 38.6 us -> none  [local(): resid_rows = lax.all_gather(resid_own, 'tp', axis=1, tiled=True)]
    ppermute x4 -> x0, starting transfers between devices: 15 us -> none  [the longest x2 11.2 us: extended(): lax.ppermute(lax.slice_in_dim(block, block.shape[dim] - width, None, axis...]
    all_to_all x1 -> x0, starting transfers between devices: 14.7 us -> none  [local(): lax.all_to_all(frames_in.reshape(shard_count, piece_rows, width), 'seq',...]
    all_to_all x1 -> x0, waiting for transfers between devices: 14.3 us -> none  [local(): lax.all_to_all(frames_in.reshape(shard_count, piece_rows, width), 'seq',...]
    ppermute x4 -> x0, waiting for transfers between devices: 6.51 us -> none  [the longest x2 6.51 us: extended(): lax.ppermute(lax.slice_in_dim(block, 0, width, axis=dim), axis, backward)]
    unnamed x29 -> x27, local copies, waits for them, and re-layouts: 8.44 us -> 8.58 us
  transfers between devices with their start and end apart: 7 -> 0, of which waited for: 5 -> 0; matrix products, arithmetic and copies ran while one was open for 1% -> 0% of each run, Pallas kernels for 0% -> 0%
where the time goes in v1:
time: 77.3 us; the launch traced here: 76.8 us
  Pallas kernels  68.2 us (88%)
  local copies, waits for them, and re-layouts  8.58 us (11%)
    pallas_call x1, Pallas kernels, local(): pl.pallas_call(block_kernel, out_shape=jax.ShapeDtypeStruct((ROWS, LW), B...  68.2 us
    unnamed x27, local copies, waits for them, and re-layouts  8.58 us

profile of v1, /device:TPU:1, one launch (start us, length us, event | category | flops | bytes accessed | tf_op | source)
XLA Modules:
  0.0 76.8 jit_solution(11551741910365901739)
XLA Ops:
  0.0 0.0 copy-start.7
  0.0 0.0 copy-start.12
  0.0 0.0 copy-start.9
  0.0 0.0 copy-start.10
  0.0 0.0 copy-start.11
  0.0 0.7 copy-done.7
  0.7 0.0 copy-done.12
  0.7 0.0 copy-done.9
  0.7 0.0 copy-done.10
  0.7 0.0 copy-done.11
  0.7 0.0 copy-start
  0.7 1.1 %copy-done = bf16[3,1024,128]{2,1,0:T(8,128)(2,1)S(1)} copy-done((bf16[3,1024,128]{2,1,0:T(8,128)(2,1)S(1)}, bf16[3,1024,128]{2,1,0:T(8,128)(2,1)}, u32[]{:S(2)}) %copy-start) | copy-done | bytes 786456
  1.9 0.0 copy-start.1
  1.9 1.0 %copy-done.1 = bf16[256,1024]{1,0:T(8,128)(2,1)S(1)} copy-done((bf16[256,1024]{1,0:T(8,128)(2,1)S(1)}, bf16[256,1024]{1,0:T(8,128)(2,1)}, u32[]{:S(2)}) %copy-start.1) | copy-done | bytes 524312
  2.9 0.0 copy-start.2
  2.9 1.0 %copy-done.2 = bf16[2,1024,128]{2,1,0:T(8,128)(2,1)S(1)} copy-done((bf16[2,1024,128]{2,1,0:T(8,128)(2,1)S(1)}, bf16[2,1024,128]{2,1,0:T(8,128)(2,1)}, u32[]{:S(2)}) %copy-start.2) | copy-done | bytes 524312
  3.9 0.0 copy-start.3
  3.9 0.9 %copy-done.3 = bf16[128,1024]{1,0:T(8,128)(2,1)S(1)} copy-done((bf16[128,1024]{1,0:T(8,128)(2,1)S(1)}, bf16[128,1024]{1,0:T(8,128)(2,1)}, u32[]{:S(2)}) %copy-start.3) | copy-done | bytes 262168
  4.9 0.0 copy-start.4
  4.9 0.9 %copy-done.4 = bf16[128,1024]{1,0:T(8,128)(2,1)S(1)} copy-done((bf16[128,1024]{1,0:T(8,128)(2,1)S(1)}, bf16[128,1024]{1,0:T(8,128)(2,1)}, u32[]{:S(2)}) %copy-start.4) | copy-done | bytes 262168
  5.8 0.0 copy-start.5
  5.8 0.8 copy-done.5
  6.6 0.0 copy-start.6
  6.6 0.7 copy-done.6
  7.3 0.0 copy-start.8
  7.3 0.7 copy-done.8
  8.0 68.2 %encoder_block.1 = bf16[256,128]{1,0:T(8,128)(2,1)S(1)} custom-call(bf16[256,1024]{1,0:T(8,128)(2,1)S(1)} %copy-done.1, s32[64,64]{1,0:T(8,128)S(1)} %copy-done.5, s32[8]{0:T(128)S(1)} %copy-done.9, s32[8]{0:T(128)S(1)} %copy-done.10, f32[1,1024]{1,0:T(1,128)S(1)} %bitcast.4, bf16[3,1024,128]{2,1,0:T(8,128)(2,1)S(1)} %copy-done, ...), custom_call_target="tpu_custom_call" | custom-call | tf_op jit(solution)/shard_map/encoder_block/pallas_call | solution.py:379
  76.2 0.6 copy.15
Async XLA Ops:
  0.0 0.7 copy-start.7
  0.0 0.7 copy-start.12
  0.0 0.7 copy-start.9
  0.0 0.7 copy-start.10
  0.0 0.7 copy-start.11
  0.7 1.1 %copy-start = (bf16[3,1024,128]{2,1,0:T(8,128)(2,1)S(1)}, bf16[3,1024,128]{2,1,0:T(8,128)(2,1)}, u32[]{:S(2)}) copy-start(bf16[3,1024,128]{2,1,0:T(8,128)(2,1)} %wqkv.1) | copy-start | bytes 2359300
  1.9 1.0 %copy-start.1 = (bf16[256,1024]{1,0:T(8,128)(2,1)S(1)}, bf16[256,1024]{1,0:T(8,128)(2,1)}, u32[]{:S(2)}) copy-start(bf16[256,1024]{1,0:T(8,128)(2,1)} %frames.1) | copy-start | bytes 1572868
  2.9 1.0 %copy-start.2 = (bf16[2,1024,128]{2,1,0:T(8,128)(2,1)S(1)}, bf16[2,1024,128]{2,1,0:T(8,128)(2,1)}, u32[]{:S(2)}) copy-start(bf16[2,1024,128]{2,1,0:T(8,128)(2,1)} %w1.1) | copy-start | bytes 1572868
  3.9 0.9 %copy-start.3 = (bf16[128,1024]{1,0:T(8,128)(2,1)S(1)}, bf16[128,1024]{1,0:T(8,128)(2,1)}, u32[]{:S(2)}) copy-start(bf16[128,1024]{1,0:T(8,128)(2,1)} %wo.1) | copy-start | bytes 786436
  4.9 0.9 %copy-start.4 = (bf16[128,1024]{1,0:T(8,128)(2,1)S(1)}, bf16[128,1024]{1,0:T(8,128)(2,1)}, u32[]{:S(2)}) copy-start(bf16[128,1024]{1,0:T(8,128)(2,1)} %w2.1) | copy-start | bytes 786436
  5.8 0.8 copy-start.5
  6.6 0.7 copy-start.6
  7.3 0.7 copy-start.8

commit v2 on v1

v2 whole, which is shorter than its diff:
```python
import functools
import math

import jax
import jax.numpy as jnp
from jax import lax
from jax.experimental import pallas as pl
from jax.experimental.pallas import tpu as pltpu
from jax.sharding import PartitionSpec as P

MESH = pl.DeviceIdType.MESH
BF16 = jnp.bfloat16
F32 = jnp.float32
I32 = jnp.int32

SEQ = 64
TP = 8
NX = 4
ROWS = 256
HALF = 128
D = 1024
LW = 128
PIECE = 4
MSG = 16
WMAX = 128
TAPS = 9
RIM = 4
EDGE = 16


def dot(a, b):
    return jnp.dot(a, b, preferred_element_type=F32)


def dot_nt(a, b):
    return lax.dot_general(a, b, (((1,), (1,)), ((), ())), preferred_element_type=F32)


def iota(shape, dim):
    return lax.broadcasted_iota(I32, shape, dim)


def one_hot(mask):
    return jnp.where(mask, 1.0, 0.0).astype(BF16)


def layer_norm(blocks, gain_ref):
    width = blocks[0].shape[1]
    mean = sum(jnp.sum(b, axis=1, keepdims=True) for b in blocks) * (1.0 / D)
    centred = [b - mean for b in blocks]
    var = sum(jnp.sum(c * c, axis=1, keepdims=True) for c in centred) * (1.0 / D)
    inv = lax.rsqrt(var + 1e-05)
    normed = [
        (c * inv * gain_ref[:, i * width : (i + 1) * width]).astype(BF16)
        for i, c in enumerate(centred)
    ]
    return jnp.concatenate(normed, axis=1)


def block_kernel(
    frames, smap_hbm, lens_hbm, wins_hbm, gain1_hbm, wqkv, wo, gain2_hbm, w1, taps_hbm,
    bn_scale_hbm, bn_shift_hbm, w2,
    out,
    smap, lens, wins, gain1, gain2, taps, bn_scale, bn_shift,
    xin, sbuf, rbuf, frame, wq, wkv, w1v, wof, w2c, qv, kvx, ctx, act, res, glu, gluf, rim,
    lo_ref, hi_ref, start_ref, end_ref,
    ld, own_sem, a2a_s, a2a_r, xs, xr, hs, hr, wos, wor, w2s, w2r, c1s, c1r, c2s, c2r, gs, gr,
):
    s = lax.axis_index("seq")
    t = lax.axis_index("tp")
    z = t // NX
    x = lax.rem(t, NX)
    core = lax.rem(s, 2)
    mate = s + 1 - 2 * core
    left = lax.rem(s + SEQ - 1, SEQ)
    right = lax.rem(s + 1, SEQ)
    z_peer = lax.rem(t + NX, TP)

    def x_peer(d):
        return z * NX + lax.rem(x + d, NX)

    def remote(src, dst, send, recv, seq, tp):
        return pltpu.make_async_remote_copy(
            src_ref=src, dst_ref=dst, send_sem=send, recv_sem=recv,
            device_id=(seq, tp), device_id_type=MESH,
        )

    flight = []
    got = []

    def post(src, dst, send, recv, seq, tp):
        cp = remote(src, dst, send, recv, seq, tp)
        cp.start()
        flight.append(cp)
        return cp

    def land(cp):
        cp.wait_recv()
        got.append(id(cp))

    def drain():
        for cp in flight:
            if id(cp) not in got:
                cp.wait_recv()
            cp.wait_send()

    parity = lax.rem(x, 2)
    quarter = 2 * parity + x // 2
    loads = []

    def load(src, dst):
        cp = pltpu.make_async_copy(src, dst, ld.at[len(loads)])
        cp.start()
        loads.append(cp)
        return cp

    ld_frames = load(frames.at[:, pl.ds(pl.multiple_of(parity * 512, 512), 512)], xin)

    bar = pltpu.get_barrier_semaphore()

    def far_first(n):
        return lax.rem(s + SEQ // 2 + ((n + 1) // 2) * (1 - 2 * lax.rem(n, 2)), SEQ)

    def greet(n, carry):
        pl.semaphore_signal(bar, inc=1, device_id=(far_first(n), t), device_id_type=MESH)
        return carry

    for d in (4, 5, 3, 6, 2, 7, 1):
        pl.semaphore_signal(bar, inc=1, device_id=(s, lax.rem(t + d, TP)), device_id_type=MESH)
    lax.fori_loop(0, SEQ - 1, greet, 0)

    ld_wo = load(wo, wof.at[pl.ds(pl.multiple_of(t * LW, LW), LW)])
    ld_map = load(smap_hbm, smap)
    ld_rec = [load(lens_hbm, lens), load(wins_hbm, wins)]
    ld_qkv = [
        load(gain1_hbm, gain1),
        load(wqkv.at[1], wkv.at[:, 0:LW]),
        load(wqkv.at[2], wkv.at[:, LW : 2 * LW]),
        load(wqkv.at[0], wq),
    ]
    ld_conv = [
        load(taps_hbm, taps), load(bn_scale_hbm, bn_scale), load(bn_shift_hbm, bn_shift)
    ]
    ld_w1 = [load(gain2_hbm, gain2), load(w1.at[0], w1v.at[:, 0:LW]), load(w1.at[1], w1v.at[:, LW : 2 * LW])]
    ld_w2 = load(
        w2.at[:, pl.ds(pl.multiple_of(t * LW, LW), LW)],
        w2c.at[pl.ds(pl.multiple_of(t * LW, LW), LW)],
    )

    ld_frames.wait()
    o = iota((256, 256), 0)
    i = iota((256, 256), 1)
    pack = one_hot(i == 64 * ((o >> 2) & 3) + 4 * (o >> 4) + (o & 3))
    unpack = one_hot(o == 64 * ((i >> 2) & 3) + 4 * (i >> 4) + (i & 3))
    for g in range(4):
        stack = jnp.concatenate(
            [xin[64 * g : 64 * g + 64, 128 * c : 128 * c + 128] for c in range(4)], axis=0
        )
        sbuf[256 * g : 256 * g + 256, :] = dot(pack, stack).astype(BF16)

    pl.semaphore_wait(bar, SEQ - 1 + TP - 1)

    def rows16(index):
        return pl.ds(pl.multiple_of(index * MSG, MSG), MSG)

    def deal(n, carry):
        j = far_first(n)
        remote(sbuf.at[rows16(j)], rbuf.at[rows16(s)], a2a_s, a2a_r, j, t).start()
        return carry

    lax.fori_loop(0, SEQ - 1, deal, 0)
    own = pltpu.make_async_copy(sbuf.at[rows16(s)], rbuf.at[rows16(s)], own_sem)
    own.start()

    def wo_rows(tp, c):
        return wof.at[pl.ds(pl.multiple_of(tp * LW + c * 64, 64), 64)]

    def wo_block(tp, c, y):
        return wof.at[
            pl.ds(pl.multiple_of(tp * LW + c * 64, 64), 64), pl.ds(pl.multiple_of(y * LW, LW), LW)
        ]

    y = s // 8
    ld_wo.wait()
    part = wo_block(t, core, y)
    wo_cross = post(part, part, wos.at[3], wor.at[3], s, z_peer)
    wo_first = []
    for d in range(1, NX):
        part = wo_rows(t, core)
        wo_first.append(post(part, part, wos.at[d - 1], wor.at[d - 1], s, x_peer(d)))

    ld_map.wait()
    col = dot_nt(one_hot(iota((8, SEQ), 1) == s), smap[...].astype(F32).astype(BF16))
    spread = one_hot((iota((SEQ, 256), 1) >> 2) == iota((SEQ, 256), 0))
    place = dot(col.astype(BF16), spread) * 4.0 + (iota((8, 256), 1) & 3).astype(F32)
    order = one_hot(place[0:1, :] == o.astype(F32))

    for cp in ld_rec:
        cp.wait()
    pos = s * ROWS + iota((ROWS, LW), 0)
    start = jnp.zeros((ROWS, LW), I32)
    end = jnp.full((ROWS, LW), SEQ * ROWS, I32)
    reach = jnp.zeros((ROWS, LW), I32)
    total = jnp.int32(0)
    for k in range(8):
        before = total
        total = total + lens[k]
        start = jnp.where(pos >= total, total, start)
        end = jnp.where(pos < total, jnp.minimum(end, total), end)
        reach = jnp.where((pos >= before) & (pos < total), wins[k], reach)
    start_ref[...] = start
    end_ref[...] = end
    lo_ref[...] = jnp.maximum(start, pos - reach)
    hi_ref[...] = jnp.minimum(end - 1, pos + reach)

    own.wait()
    wait_all = remote(
        sbuf.at[0 : MSG * (SEQ - 1)], rbuf.at[0 : MSG * (SEQ - 1)], a2a_s, a2a_r, right, t
    )
    wait_all.wait_recv()
    parts = [dot(unpack, rbuf[256 * g : 256 * g + 256, :]).astype(BF16) for g in range(4)]
    dealt = jnp.concatenate(
        [
            jnp.concatenate([parts[g][64 * c : 64 * c + 64] for g in range(4)], axis=0)
            for c in range(4)
        ],
        axis=1,
    )
    ordered = dot(order, dealt).astype(BF16)
    frame[2 * parity] = ordered[:, 0:256]
    frame[2 * parity + 1] = ordered[:, 256:512]

    swaps = []
    for c in range(2):
        pair = []
        for n, d in enumerate((1, 3)):
            part = frame.at[quarter, c * HALF : (c + 1) * HALF]
            cp = post(part, part, xs.at[c, n], xr.at[c, n], s, x_peer(d))
            pair.append(cp)
        swaps.append(pair)

    land(wo_cross)
    wo_share = []
    for d in (4, 3, 5, 2, 6, 1, 7):
        part = wo_block(z_peer, core, y)
        k = 13 + d
        wo_share.append(post(part, part, wos.at[k], wor.at[k], lax.rem(s + 8 * d, SEQ), t))

    for cp in ld_qkv:
        cp.wait()
    halos = []
    for c in range(2):
        for cp in swaps[c]:
            land(cp)
        rows = slice(c * HALF, (c + 1) * HALF)
        z1 = layer_norm([frame[q, rows, :].astype(F32) for q in range(4)], gain1)
        kvx[WMAX + c * HALF : WMAX + (c + 1) * HALF, :] = dot(z1, wkv[...]).astype(BF16)
        src = kvx.at[WMAX + c * HALF : WMAX + (c + 1) * HALF]
        if c == 0:
            cp = post(src, kvx.at[WMAX + ROWS : 2 * WMAX + ROWS], hs.at[0], hr.at[0], left, t)
        else:
            cp = post(src, kvx.at[0:WMAX], hs.at[1], hr.at[1], right, t)
        halos.append(cp)
        qv[rows, :] = dot(z1, wq[...]).astype(BF16)

    for cp in wo_share:
        land(cp)
    wo_next = []
    for d in range(1, NX):
        cp = post(
            wo_rows(z_peer, core), wo_rows(z_peer, core), wos.at[3 + d], wor.at[3 + d], s, x_peer(d)
        )
        wo_next.append(cp)
    wo_swap = []

    def give_wo(tp):
        k = 7 + len(wo_swap)
        cp = post(wo_rows(tp, core), wo_rows(tp, core), wos.at[k], wor.at[k], mate, t)
        wo_swap.append(cp)

    give_wo(z_peer)
    for d in range(1, NX):
        land(wo_first[d - 1])
        give_wo(x_peer(NX - d))

    def send_group(buf, rows, send, recv):
        sent = []
        for k, peer in enumerate([z_peer, x_peer(1), x_peer(2), x_peer(3)]):
            cp = post(buf.at[t, rows], buf.at[t, rows], send.at[k], recv.at[k], s, peer)
            sent.append(cp)
        return sent

    def pass_on(buf, rows, send, recv, sent):
        land(sent[0])
        for d in range(1, NX):
            cp = post(
                buf.at[z_peer, rows], buf.at[z_peer, rows], send.at[3 + d], recv.at[3 + d],
                s, x_peer(d),
            )
            sent.append(cp)

    def whole(buf, rows, sent):
        for cp in sent[1:]:
            land(cp)
        return jnp.concatenate([buf[k, rows, :] for k in range(TP)], axis=1)

    EDGES = (slice(192, 256), slice(0, 64))
    PLACES = (slice(0, HALF), slice(HALF, ROWS))

    def natural(ref_rows, c):
        if c == 1:
            return ref_rows(slice(64, 192))
        return jnp.concatenate([ref_rows(e) for e in EDGES], axis=0)

    scale = 1.0 / math.sqrt(LW)

    def masked_scores(c, first, count):
        rows = slice(c * HALF, (c + 1) * HALF)
        scores = dot_nt(qv[rows, :], kvx[first : first + count, 0:LW]) * scale
        kpos = s * ROWS + first - WMAX + iota((HALF, count), 1)
        low = jnp.concatenate([lo_ref[rows, :]] * (count // LW), axis=1)
        high = jnp.concatenate([hi_ref[rows, :]] * (count // LW), axis=1)
        return jnp.where((kpos >= low) & (kpos <= high), scores, -1e30)

    def attend_own(c):
        scores = masked_scores(c, WMAX, ROWS)
        peak = jnp.max(scores, axis=1, keepdims=True)
        weights = jnp.exp(scores - peak)
        total = jnp.sum(weights, axis=1, keepdims=True)
        return peak, total, dot(weights.astype(BF16), kvx[WMAX : WMAX + ROWS, LW : 2 * LW])

    own_part = {c: attend_own(c) for c in (1, 0)}
    for c in (1, 0):
        first = 0 if c == 0 else WMAX + ROWS
        land(halos[1 - c])
        scores = masked_scores(c, first, WMAX)
        own_peak, own_total, own_sum = own_part[c]
        peak = jnp.maximum(own_peak, jnp.max(scores, axis=1, keepdims=True))
        weights = jnp.exp(scores - peak)
        fade = jnp.exp(own_peak - peak)
        total = own_total * fade + jnp.sum(weights, axis=1, keepdims=True)
        mixed = own_sum * fade + dot(weights.astype(BF16), kvx[first : first + WMAX, LW : 2 * LW])
        mixed = (mixed / total).astype(BF16)
        if c == 1:
            ctx[t, 0:64, :] = mixed[64:128]
            ctx[t, 192:256, :] = mixed[0:64]
        else:
            ctx[t, 64:192, :] = mixed
    sent1 = {}
    for c in (0, 1):
        sent1[c] = send_group(ctx, PLACES[c], c1s.at[c], c1r.at[c])

    for d in range(1, NX):
        land(wo_next[d - 1])
        give_wo(lax.rem(x_peer(NX - d) + NX, TP))
    for c in (0, 1):
        pass_on(ctx, PLACES[c], c1s.at[c], c1r.at[c], sent1[c])

    w2_first = []
    for k in (4, 5, 3, 6, 2, 7, 1):
        peer = lax.rem(t + k, TP)
        w2_first.append(
            post(
                w2.at[
                    pl.ds(pl.multiple_of(core * 64, 64), 64), pl.ds(pl.multiple_of(peer * LW, LW), LW)
                ],
                w2c.at[pl.ds(pl.multiple_of(t * LW + core * 64, 64), 64)],
                w2s.at[k - 1], w2r.at[k - 1], s, peer,
            )
        )

    for cp in wo_swap:
        land(cp)
    for cp in ld_w1:
        cp.wait()

    def conv_act(first, count):
        rows = slice(first, first + count)
        at = s * ROWS + first + iota((count, LW), 0)
        room_low = start_ref[rows, :] - at
        room_high = end_ref[rows, :] - at
        conv = jnp.zeros((count, LW), F32)
        for k in range(TAPS):
            begin = EDGE + first + k - RIM
            valid = (room_low <= k - RIM) & (room_high > k - RIM)
            conv = conv + jnp.where(valid, gluf[begin : begin + count, :] * taps[k : k + 1, :], 0.0)
        shifted = conv * bn_scale[...] + bn_shift[...]
        return (shifted * jax.nn.sigmoid(shifted)).astype(BF16)

    edges = []
    for c in (0, 1):
        attn = dot(whole(ctx, PLACES[c], sent1[c]), wof[...])
        resid = [
            (
                natural(lambda rows: frame[q, rows, :], c).astype(F32)
                + attn[:, 256 * q : 256 * q + 256]
            ).astype(BF16)
            for q in range(4)
        ]
        for q in range(4):
            res[2 * q, PLACES[c], :] = resid[q][:, 0:LW]
            res[2 * q + 1, PLACES[c], :] = resid[q][:, LW : 2 * LW]
        z2 = layer_norm([r.astype(F32) for r in resid], gain2)
        both = dot(z2, w1v[...])
        gated = (both[:, 0:LW] * jax.nn.sigmoid(both[:, LW : 2 * LW])).astype(BF16)
        if c == 0:
            glu[0] = gated[64 - EDGE : 64]
            glu[1] = gated[64 : 64 + EDGE]
            edges.append(post(glu.at[0], rim.at[0], gs.at[0], gr.at[0], right, t))
            edges.append(post(glu.at[1], rim.at[1], gs.at[1], gr.at[1], left, t))
            gluf[EDGE + 192 : EDGE + 256, :] = gated[0:64].astype(F32)
            gluf[EDGE : EDGE + 64, :] = gated[64:128].astype(F32)
        else:
            gluf[EDGE + 64 : EDGE + 192, :] = gated.astype(F32)

    sent2 = {}
    for cp in ld_conv:
        cp.wait()
    act[t, PLACES[1], :] = conv_act(64, HALF)
    sent2[1] = send_group(act, PLACES[1], c2s.at[1], c2r.at[1])
    land(edges[0])
    gluf[0:EDGE, :] = rim[0].astype(F32)
    land(edges[1])
    gluf[EDGE + ROWS : 2 * EDGE + ROWS, :] = rim[1].astype(F32)
    act[t, 0:64, :] = conv_act(192, 64)
    act[t, 64:128, :] = conv_act(0, 64)
    sent2[0] = send_group(act, PLACES[0], c2s.at[0], c2r.at[0])

    w2_swap = []
    for i, k in enumerate((4, 5, 3, 6, 2, 7, 1)):
        land(w2_first[i])
        part = w2c.at[pl.ds(pl.multiple_of(lax.rem(t + TP - k, TP) * LW + core * 64, 64), 64)]
        w2_swap.append(post(part, part, w2s.at[6 + k], w2r.at[6 + k], mate, t))
    for c in (1, 0):
        pass_on(act, PLACES[c], c2s.at[c], c2r.at[c], sent2[c])
    ld_w2.wait()
    for cp in w2_swap:
        land(cp)
    for c in (1, 0):
        summed = dot(whole(act, PLACES[c], sent2[c]), w2c[...])
        final = (res[t, PLACES[c], :].astype(F32) + summed).astype(BF16)
        if c == 1:
            out[64:192, :] = final
        else:
            out[192:256, :] = final[0:64]
            out[0:64, :] = final[64:128]

    wait_all.wait_send()
    drain()


def local(
    frames_in, stretch_map, rec_lengths, windows, ln1_gain, wqkv, wo, ln2_gain, w1,
    dw_kernel, bn_scale, bn_shift, w2,
):
    vmem = pl.BlockSpec(memory_space=pltpu.VMEM)
    hbm = pl.BlockSpec(memory_space=pl.ANY)
    dma = pltpu.SemaphoreType.DMA
    return pl.pallas_call(
        block_kernel,
        out_shape=jax.ShapeDtypeStruct((ROWS, LW), BF16),
        in_specs=[hbm] * 13,
        out_specs=vmem,
        scratch_shapes=[
            pltpu.VMEM((SEQ, SEQ), I32),
            pltpu.SMEM((8,), I32),
            pltpu.SMEM((8,), I32),
            pltpu.VMEM((1, D), F32),
            pltpu.VMEM((1, D), F32),
            pltpu.VMEM((TAPS, LW), F32),
            pltpu.VMEM((1, LW), F32),
            pltpu.VMEM((1, LW), F32),
            pltpu.VMEM((ROWS, 512), BF16),
            pltpu.VMEM((SEQ * MSG, 128), BF16),
            pltpu.VMEM((SEQ * MSG, 128), BF16),
            pltpu.VMEM((4, ROWS, 256), BF16),
            pltpu.VMEM((D, LW), BF16),
            pltpu.VMEM((D, 2 * LW), BF16),
            pltpu.VMEM((D, 2 * LW), BF16),
            pltpu.VMEM((D, D), BF16),
            pltpu.VMEM((D, LW), BF16),
            pltpu.VMEM((ROWS, LW), BF16),
            pltpu.VMEM((ROWS + 2 * WMAX, 2 * LW), BF16),
            pltpu.VMEM((TP, ROWS, LW), BF16),
            pltpu.VMEM((TP, ROWS, LW), BF16),
            pltpu.VMEM((TP, ROWS, LW), BF16),
            pltpu.VMEM((2, EDGE, LW), BF16),
            pltpu.VMEM((ROWS + 2 * EDGE, LW), F32),
            pltpu.VMEM((2, EDGE, LW), BF16),
            pltpu.VMEM((ROWS, LW), I32),
            pltpu.VMEM((ROWS, LW), I32),
            pltpu.VMEM((ROWS, LW), I32),
            pltpu.VMEM((ROWS, LW), I32),
            dma((16,)),
            dma,
            dma,
            dma,
            dma((2, 2)),
            dma((2, 2)),
            dma((2,)),
            dma((2,)),
            dma((21,)),
            dma((21,)),
            dma((14,)),
            dma((14,)),
            dma((2, 7)),
            dma((2, 7)),
            dma((2, 7)),
            dma((2, 7)),
            dma((2,)),
            dma((2,)),
        ],
        compiler_params=pltpu.CompilerParams(
            collective_id=0, has_side_effects=True, vmem_limit_bytes=60 << 20
        ),
        name="encoder_block",
    )(
        frames_in, stretch_map, rec_lengths, windows, ln1_gain.reshape(1, D), wqkv, wo,
        ln2_gain.reshape(1, D), w1, dw_kernel, bn_scale.reshape(1, LW),
        bn_shift.reshape(1, LW), w2,
    )


def solution(mesh):
    placed = (
        P("seq", None),
        P(),
        P(),
        P(),
        P(),
        P(None, None, "tp"),
        P("tp", None),
        P(),
        P(None, None, "tp"),
        P(None, "tp"),
        P("tp"),
        P("tp"),
        P("tp", None),
    )
    return jax.shard_map(
        local, mesh=mesh, in_specs=placed, out_specs=P("seq", "tp"), check_vma=False
    )
```

time: 77.3 us -> 60.9 us (0.79)
  Pallas kernels: 68.2 us -> 59.1 us
  local copies, waits for them, and re-layouts: 8.58 us -> 1.47 us
    pallas_call x1, Pallas kernels: 68.2 us -> 59.1 us  [local(): pl.pallas_call(block_kernel, out_shape=jax.ShapeDtypeStruct((ROWS, LW), B...]
    unnamed x27 -> x1, local copies, waits for them, and re-layouts: 8.58 us -> 1.47 us
where the time goes in v2:
time: 60.9 us; the launch traced here: 60.6 us
  Pallas kernels  59.1 us (97%)
  local copies, waits for them, and re-layouts  1.47 us (2%)
    pallas_call x1, Pallas kernels, local(): pl.pallas_call(block_kernel, out_shape=jax.ShapeDtypeStruct((ROWS, LW), B...  59.1 us
    unnamed x1, local copies, waits for them, and re-layouts  1.47 us

profile of v2, /device:TPU:1, one launch (start us, length us, event | category | flops | bytes accessed | tf_op | source)
XLA Modules:
  0.0 60.6 jit_solution(4015550219581221089)
XLA Ops:
  0.0 59.1 %encoder_block.1 = bf16[256,128]{1,0:T(8,128)(2,1)} custom-call(bf16[256,1024]{1,0:T(8,128)(2,1)} %frames.1, s32[64,64]{1,0:T(8,128)} %smap_hbm.1, s32[8]{0:T(128)} %lens_hbm.1, s32[8]{0:T(128)} %wins_hbm.1, f32[1,1024]{1,0:T(1,128)} %bitcast.4, bf16[3,1024,128]{2,1,0:T(8,128)(2,1)} %wqkv.1, bf16[128,1024]{1,0:T(8,128)(2,1)} %wo.1, f32[1,1024]{1,0:T(1,128)} %bitcast.5, ...), custom_call_target="tpu_custom_call" | custom-call | tf_op jit(solution)/shard_map/encoder_block/pallas_call | solution.py:459
  59.1 1.5 %copy.15 = bf16[256,128]{1,0:T(8,128)(2,1)} copy(bf16[256,128]{1,0:T(8,128)(2,1)} %encoder_block.1) | data formatting | bytes 131072

commit v3 on v2

--- a/solution.py
+++ b/solution.py
@@ -21,7 +21,7 @@
 D = 1024
 LW = 128
 PIECE = 4
-MSG = 16
+MSG = 8
 WMAX = 128
 TAPS = 9
 RIM = 4
@@ -62,9 +62,9 @@
     bn_scale_hbm, bn_shift_hbm, w2,
     out,
     smap, lens, wins, gain1, gain2, taps, bn_scale, bn_shift,
-    xin, sbuf, rbuf, frame, wq, wkv, w1v, wof, w2c, qv, kvx, ctx, act, res, glu, gluf, rim,
+    outv, xin, sbuf, rbuf, order, frame, wq, wkv, w1v, wof, w2c, qv, kvx, ctx, act, res, glu, gluf, rim,
     lo_ref, hi_ref, start_ref, end_ref,
-    ld, own_sem, a2a_s, a2a_r, xs, xr, hs, hr, wos, wor, w2s, w2r, c1s, c1r, c2s, c2r, gs, gr,
+    ld, out_sem, own_sem, a2a_s, a2a_r, xs, xr, hs, hr, wos, wor, w2s, w2r, c1s, c1r, c2s, c2r, gs, gr,
 ):
     s = lax.axis_index("seq")
     t = lax.axis_index("tp")
@@ -114,7 +114,11 @@
         loads.append(cp)
         return cp
 
-    ld_frames = load(frames.at[:, pl.ds(pl.multiple_of(parity * 512, 512), 512)], xin)
+    kept = 2 * parity + 1 - x // 2
+    ld_frames = [
+        load(frames.at[:, pl.ds(pl.multiple_of(q * 256, 256), 256)], xin.at[b])
+        for b, q in enumerate((quarter, kept))
+    ]
 
     bar = pltpu.get_barrier_semaphore()
 
@@ -147,30 +151,25 @@
         w2c.at[pl.ds(pl.multiple_of(t * LW, LW), LW)],
     )
 
-    ld_frames.wait()
-    o = iota((256, 256), 0)
-    i = iota((256, 256), 1)
-    pack = one_hot(i == 64 * ((o >> 2) & 3) + 4 * (o >> 4) + (o & 3))
-    unpack = one_hot(o == 64 * ((i >> 2) & 3) + 4 * (i >> 4) + (i & 3))
+    for cp in ld_frames:
+        cp.wait()
+    o = iota((HALF, HALF), 0)
+    pack = one_hot(iota((HALF, HALF), 1) == 64 * ((o >> 2) & 1) + 4 * (o >> 3) + (o & 3))
     for g in range(4):
+        rows = slice(64 * g, 64 * g + 64)
         stack = jnp.concatenate(
-            [xin[64 * g : 64 * g + 64, 128 * c : 128 * c + 128] for c in range(4)], axis=0
+            [
+                jnp.concatenate([xin[b, rows, 0:128], xin[b, rows, 128:256]], axis=0)
+                for b in range(2)
+            ],
+            axis=1,
         )
-        sbuf[256 * g : 256 * g + 256, :] = dot(pack, stack).astype(BF16)
+        packed = dot(pack, stack)
+        for b in range(2):
+            part = packed[:, 128 * b : 128 * b + 128].reshape(16, MSG, 128)
+            sbuf[b, 16 * g : 16 * g + 16] = part.astype(BF16)
 
     pl.semaphore_wait(bar, SEQ - 1 + TP - 1)
-
-    def rows16(index):
-        return pl.ds(pl.multiple_of(index * MSG, MSG), MSG)
-
-    def deal(n, carry):
-        j = far_first(n)
-        remote(sbuf.at[rows16(j)], rbuf.at[rows16(s)], a2a_s, a2a_r, j, t).start()
-        return carry
-
-    lax.fori_loop(0, SEQ - 1, deal, 0)
-    own = pltpu.make_async_copy(sbuf.at[rows16(s)], rbuf.at[rows16(s)], own_sem)
-    own.start()
 
     def wo_rows(tp, c):
         return wof.at[pl.ds(pl.multiple_of(tp * LW + c * 64, 64), 64)]
@@ -189,11 +188,33 @@
         part = wo_rows(t, core)
         wo_first.append(post(part, part, wos.at[d - 1], wor.at[d - 1], s, x_peer(d)))
 
+    own = []
+    deals = []
+    for b in range(2):
+
+        def deal(n, carry):
+            j = far_first(n)
+            remote(sbuf.at[b, j], rbuf.at[b, s], a2a_s.at[b], a2a_r.at[b], j, t).start()
+            return carry
+
+        lax.fori_loop(0, SEQ - 1, deal, 0)
+        cp = pltpu.make_async_copy(sbuf.at[b, s], rbuf.at[b, s], own_sem.at[b])
+        cp.start()
+        own.append(cp)
+        deals.append(
+            remote(
+                sbuf.at[b, 0 : SEQ - 1], rbuf.at[b, 0 : SEQ - 1], a2a_s.at[b], a2a_r.at[b], right, t
+            )
+        )
+
     ld_map.wait()
     col = dot_nt(one_hot(iota((8, SEQ), 1) == s), smap[...].astype(F32).astype(BF16))
-    spread = one_hot((iota((SEQ, 256), 1) >> 2) == iota((SEQ, 256), 0))
-    place = dot(col.astype(BF16), spread) * 4.0 + (iota((8, 256), 1) & 3).astype(F32)
-    order = one_hot(place[0:1, :] == o.astype(F32))
+    i = iota((8, SEQ * MSG), 1)
+    spread = one_hot((iota((SEQ, SEQ * MSG), 1) >> 3) == iota((SEQ, SEQ * MSG), 0))
+    place = dot(col.astype(BF16), spread) * 4.0 + (i & 3).astype(F32)
+    o = iota((ROWS, SEQ * MSG), 0).astype(F32)
+    for c in range(2):
+        order[c] = one_hot(jnp.where(((i >> 2) & 1) == c, place, -1.0)[0:1, :] == o)
 
     for cp in ld_rec:
         cp.wait()
@@ -213,38 +234,35 @@
     lo_ref[...] = jnp.maximum(start, pos - reach)
     hi_ref[...] = jnp.minimum(end - 1, pos + reach)
 
-    own.wait()
-    wait_all = remote(
-        sbuf.at[0 : MSG * (SEQ - 1)], rbuf.at[0 : MSG * (SEQ - 1)], a2a_s, a2a_r, right, t
-    )
-    wait_all.wait_recv()
-    parts = [dot(unpack, rbuf[256 * g : 256 * g + 256, :]).astype(BF16) for g in range(4)]
-    dealt = jnp.concatenate(
-        [
-            jnp.concatenate([parts[g][64 * c : 64 * c + 64] for g in range(4)], axis=0)
-            for c in range(4)
-        ],
-        axis=1,
-    )
-    ordered = dot(order, dealt).astype(BF16)
-    frame[2 * parity] = ordered[:, 0:256]
-    frame[2 * parity + 1] = ordered[:, 256:512]
-
+    def settle(b, q):
+        own[b].wait()
+        deals[b].wait_recv()
+        dealt = rbuf[b].astype(F32).reshape(SEQ * MSG, 128).astype(BF16)
+        for c in range(2):
+            frame[q, :, 128 * c : 128 * c + 128] = dot(order[c], dealt).astype(BF16)
+
+    land(wo_cross)
+    part = wo_block(z_peer, core, y)
+    wo_opposite = post(part, part, wos.at[4], wor.at[4], s, x_peer(2))
+
+    settle(0, quarter)
     swaps = []
     for c in range(2):
         pair = []
         for n, d in enumerate((1, 3)):
             part = frame.at[quarter, c * HALF : (c + 1) * HALF]
-            cp = post(part, part, xs.at[c, n], xr.at[c, n], s, x_peer(d))
-            pair.append(cp)
+            pair.append(post(part, part, xs.at[c, n], xr.at[c, n], s, x_peer(d)))
         swaps.append(pair)
-
-    land(wo_cross)
-    wo_share = []
-    for d in (4, 3, 5, 2, 6, 1, 7):
-        part = wo_block(z_peer, core, y)
-        k = 13 + d
-        wo_share.append(post(part, part, wos.at[k], wor.at[k], lax.rem(s + 8 * d, SEQ), t))
+    settle(1, kept)
+
+    def share(tp, first):
+        part = wo_block(tp, core, y)
+        return [
+            post(part, part, wos.at[first + d], wor.at[first + d], lax.rem(s + 8 * d, SEQ), t)
+            for d in (4, 3, 5, 2, 6, 1, 7)
+        ]
+
+    wo_share = share(z_peer, 13)
 
     for cp in ld_qkv:
         cp.wait()
@@ -266,11 +284,9 @@
     for cp in wo_share:
         land(cp)
     wo_next = []
-    for d in range(1, NX):
-        cp = post(
-            wo_rows(z_peer, core), wo_rows(z_peer, core), wos.at[3 + d], wor.at[3 + d], s, x_peer(d)
-        )
-        wo_next.append(cp)
+    for n, d in enumerate((1, 3)):
+        part = wo_rows(z_peer, core)
+        wo_next.append(post(part, part, wos.at[5 + n], wor.at[5 + n], s, x_peer(d)))
     wo_swap = []
 
     def give_wo(tp):
@@ -283,12 +299,13 @@
         land(wo_first[d - 1])
         give_wo(x_peer(NX - d))
 
-    def send_group(buf, rows, send, recv):
-        sent = []
-        for k, peer in enumerate([z_peer, x_peer(1), x_peer(2), x_peer(3)]):
-            cp = post(buf.at[t, rows], buf.at[t, rows], send.at[k], recv.at[k], s, peer)
-            sent.append(cp)
-        return sent
+    x_peers = [x_peer(1), x_peer(2), x_peer(3)]
+
+    def send_group(buf, rows, send, recv, peers, first):
+        return [
+            post(buf.at[t, rows], buf.at[t, rows], send.at[k], recv.at[k], s, peer)
+            for k, peer in enumerate(peers, first)
+        ]
 
     def pass_on(buf, rows, send, recv, sent):
         land(sent[0])
@@ -299,13 +316,23 @@
             )
             sent.append(cp)
 
+    def send_direct(buf, rows, send, recv):
+        return [
+            post(
+                buf.at[t, rows], buf.at[t, rows], send.at[k], recv.at[k], s, lax.rem(t + d, TP)
+            )
+            for k, d in enumerate((4, 5, 3, 6, 2, 7, 1))
+        ]
+
     def whole(buf, rows, sent):
-        for cp in sent[1:]:
-            land(cp)
+        for cp in sent:
+            if id(cp) not in got:
+                land(cp)
         return jnp.concatenate([buf[k, rows, :] for k in range(TP)], axis=1)
 
     EDGES = (slice(192, 256), slice(0, 64))
-    PLACES = (slice(0, HALF), slice(HALF, ROWS))
+    PLACES = (slice(0, HALF), slice(HALF, 192))
+    BLOCKS = (slice(0, HALF), slice(HALF, ROWS))
 
     def natural(ref_rows, c):
         if c == 1:
@@ -348,10 +375,17 @@
             ctx[t, 64:192, :] = mixed
     sent1 = {}
     for c in (0, 1):
-        sent1[c] = send_group(ctx, PLACES[c], c1s.at[c], c1r.at[c])
-
-    for d in range(1, NX):
-        land(wo_next[d - 1])
+        sent1[c] = send_group(ctx, PLACES[c], c1s.at[c], c1r.at[c], [z_peer], 0)
+    for c in (0, 1):
+        sent1[c] += send_group(ctx, PLACES[c], c1s.at[c], c1r.at[c], x_peers, 1)
+    straight = send_direct(ctx, slice(192, 256), c1s.at[2], c1r.at[2])
+
+    z_opposite = lax.rem(x_peer(2) + NX, TP)
+    land(wo_opposite)
+    wo_share_opposite = share(z_opposite, 20)
+
+    for n, d in enumerate((1, 3)):
+        land(wo_next[n])
         give_wo(lax.rem(x_peer(NX - d) + NX, TP))
     for c in (0, 1):
         pass_on(ctx, PLACES[c], c1s.at[c], c1r.at[c], sent1[c])
@@ -369,6 +403,9 @@
             )
         )
 
+    for cp in wo_share_opposite:
+        land(cp)
+    give_wo(z_opposite)
     for cp in wo_swap:
         land(cp)
     for cp in ld_w1:
@@ -389,7 +426,7 @@
 
     edges = []
     for c in (0, 1):
-        attn = dot(whole(ctx, PLACES[c], sent1[c]), wof[...])
+        attn = dot(whole(ctx, BLOCKS[c], sent1[c] + straight * c), wof[...])
         resid = [
             (
                 natural(lambda rows: frame[q, rows, :], c).astype(F32)
@@ -398,8 +435,13 @@
             for q in range(4)
         ]
         for q in range(4):
-            res[2 * q, PLACES[c], :] = resid[q][:, 0:LW]
-            res[2 * q + 1, PLACES[c], :] = resid[q][:, LW : 2 * LW]
+            for half in range(2):
+                part = resid[q][:, half * LW : (half + 1) * LW]
+                if c == 0:
+                    res[2 * q + half, 192:256, :] = part[0:64]
+                    res[2 * q + half, 0:64, :] = part[64:128]
+                else:
+                    res[2 * q + half, 64:192, :] = part
         z2 = layer_norm([r.astype(F32) for r in resid], gain2)
         both = dot(z2, w1v[...])
         gated = (both[:, 0:LW] * jax.nn.sigmoid(both[:, LW : 2 * LW])).astype(BF16)
@@ -413,39 +455,51 @@
         else:
             gluf[EDGE + 64 : EDGE + 192, :] = gated.astype(F32)
 
-    sent2 = {}
     for cp in ld_conv:
         cp.wait()
-    act[t, PLACES[1], :] = conv_act(64, HALF)
-    sent2[1] = send_group(act, PLACES[1], c2s.at[1], c2r.at[1])
+    PIECES = ((0, 80), (80, 160), (160, 224))
+    sent2 = []
+    for n, (begin, stop) in enumerate(PIECES):
+        act[t, begin:stop, :] = conv_act(EDGE + begin, stop - begin)
+        sent2.append(
+            send_group(act, slice(begin, stop), c2s.at[n], c2r.at[n], [z_peer], 0)
+        )
+    for n, (begin, stop) in enumerate(PIECES):
+        sent2[n] += send_group(act, slice(begin, stop), c2s.at[n], c2r.at[n], x_peers, 1)
     land(edges[0])
     gluf[0:EDGE, :] = rim[0].astype(F32)
     land(edges[1])
     gluf[EDGE + ROWS : 2 * EDGE + ROWS, :] = rim[1].astype(F32)
-    act[t, 0:64, :] = conv_act(192, 64)
-    act[t, 64:128, :] = conv_act(0, 64)
-    sent2[0] = send_group(act, PLACES[0], c2s.at[0], c2r.at[0])
+    act[t, 224:240, :] = conv_act(ROWS - EDGE, EDGE)
+    act[t, 240:256, :] = conv_act(0, EDGE)
+    last = send_direct(act, slice(224, 256), c2s.at[3], c2r.at[3])
 
     w2_swap = []
-    for i, k in enumerate((4, 5, 3, 6, 2, 7, 1)):
-        land(w2_first[i])
+    for n, k in enumerate((4, 5, 3, 6, 2, 7, 1)):
+        land(w2_first[n])
         part = w2c.at[pl.ds(pl.multiple_of(lax.rem(t + TP - k, TP) * LW + core * 64, 64), 64)]
         w2_swap.append(post(part, part, w2s.at[6 + k], w2r.at[6 + k], mate, t))
-    for c in (1, 0):
-        pass_on(act, PLACES[c], c2s.at[c], c2r.at[c], sent2[c])
+    for n, (begin, stop) in enumerate(PIECES):
+        pass_on(act, slice(begin, stop), c2s.at[n], c2r.at[n], sent2[n])
     ld_w2.wait()
     for cp in w2_swap:
         land(cp)
-    for c in (1, 0):
-        summed = dot(whole(act, PLACES[c], sent2[c]), w2c[...])
-        final = (res[t, PLACES[c], :].astype(F32) + summed).astype(BF16)
-        if c == 1:
-            out[64:192, :] = final
-        else:
-            out[192:256, :] = final[0:64]
-            out[0:64, :] = final[64:128]
-
-    wait_all.wait_send()
+
+    def finish(first, count, begin, sent):
+        summed = dot(whole(act, slice(begin, begin + count), sent), w2c[...])
+        rows = slice(first, first + count)
+        outv[rows, :] = (res[t, rows, :].astype(F32) + summed).astype(BF16)
+
+    for n, (begin, stop) in enumerate(PIECES):
+        finish(EDGE + begin, stop - begin, begin, sent2[n])
+    finish(ROWS - EDGE, EDGE, 224, last)
+    finish(0, EDGE, 240, last)
+    cp = pltpu.make_async_copy(outv, out, out_sem)
+    cp.start()
+    cp.wait()
+
+    for cp in deals:
+        cp.wait_send()
     drain()
 
 
@@ -453,14 +507,13 @@
     frames_in, stretch_map, rec_lengths, windows, ln1_gain, wqkv, wo, ln2_gain, w1,
     dw_kernel, bn_scale, bn_shift, w2,
 ):
-    vmem = pl.BlockSpec(memory_space=pltpu.VMEM)
     hbm = pl.BlockSpec(memory_space=pl.ANY)
     dma = pltpu.SemaphoreType.DMA
     return pl.pallas_call(
         block_kernel,
         out_shape=jax.ShapeDtypeStruct((ROWS, LW), BF16),
         in_specs=[hbm] * 13,
-        out_specs=vmem,
+        out_specs=hbm,
         scratch_shapes=[
             pltpu.VMEM((SEQ, SEQ), I32),
             pltpu.SMEM((8,), I32),
@@ -470,9 +523,11 @@
             pltpu.VMEM((TAPS, LW), F32),
             pltpu.VMEM((1, LW), F32),
             pltpu.VMEM((1, LW), F32),
-            pltpu.VMEM((ROWS, 512), BF16),
-            pltpu.VMEM((SEQ * MSG, 128), BF16),
-            pltpu.VMEM((SEQ * MSG, 128), BF16),
+            pltpu.VMEM((ROWS, LW), BF16),
+            pltpu.VMEM((2, ROWS, 256), BF16),
+            pltpu.VMEM((2, SEQ, MSG, 128), BF16),
+            pltpu.VMEM((2, SEQ, MSG, 128), BF16),
+            pltpu.VMEM((2, ROWS, SEQ * MSG), BF16),
             pltpu.VMEM((4, ROWS, 256), BF16),
             pltpu.VMEM((D, LW), BF16),
             pltpu.VMEM((D, 2 * LW), BF16),
@@ -491,22 +546,23 @@
             pltpu.VMEM((ROWS, LW), I32),
             pltpu.VMEM((ROWS, LW), I32),
             pltpu.VMEM((ROWS, LW), I32),
-            dma((16,)),
+            dma((17,)),
             dma,
-            dma,
-            dma,
+            dma((2,)),
+            dma((2,)),
+            dma((2,)),
             dma((2, 2)),
             dma((2, 2)),
             dma((2,)),
             dma((2,)),
-            dma((21,)),
-            dma((21,)),
+            dma((28,)),
+            dma((28,)),
             dma((14,)),
             dma((14,)),
-            dma((2, 7)),
-            dma((2, 7)),
-            dma((2, 7)),
-            dma((2, 7)),
+            dma((3, 7)),
+            dma((3, 7)),
+            dma((4, 7)),
+            dma((4, 7)),
             dma((2,)),
             dma((2,)),
         ],

time: 60.9 us -> 58.9 us (0.967)
  the two profiles are of different devices: /device:TPU:1 before, /device:TPU:32 now
where the time goes in v3:
time: 58.9 us; the launch traced here: 58.8 us
  Pallas kernels  57.3 us (97%)
  local copies, waits for them, and re-layouts  1.47 us (2%)
    pallas_call x1, Pallas kernels, local(): pl.pallas_call(block_kernel, out_shape=jax.ShapeDtypeStruct((ROWS, LW), B...  57.3 us
    unnamed x1, local copies, waits for them, and re-layouts  1.47 us

profile of v3, /device:TPU:32, one launch (start us, length us, event | category | flops | bytes accessed | tf_op | source)
XLA Modules:
  0.0 58.8 jit_solution(16849686727119938223)
XLA Ops:
  0.0 57.3 %encoder_block.1 = bf16[256,128]{1,0:T(8,128)(2,1)} custom-call(bf16[256,1024]{1,0:T(8,128)(2,1)} %frames.1, s32[64,64]{1,0:T(8,128)} %smap_hbm.1, s32[8]{0:T(128)} %lens_hbm.1, s32[8]{0:T(128)} %wins_hbm.1, f32[1,1024]{1,0:T(1,128)} %bitcast.4, bf16[3,1024,128]{2,1,0:T(8,128)(2,1)} %wqkv.1, bf16[128,1024]{1,0:T(8,128)(2,1)} %wo.1, f32[1,1024]{1,0:T(1,128)} %bitcast.5, ...), custom_call_target="tpu_custom_call" | custom-call | tf_op jit(solution)/shard_map/encoder_block/pallas_call | solution.py:512
  57.3 1.5 %copy.15 = bf16[256,128]{1,0:T(8,128)(2,1)} copy(bf16[256,128]{1,0:T(8,128)(2,1)} %encoder_block.1) | data formatting | bytes 131072

commit v4 on v3

--- a/solution.py
+++ b/solution.py
@@ -246,13 +246,16 @@
     wo_opposite = post(part, part, wos.at[4], wor.at[4], s, x_peer(2))
 
     settle(0, quarter)
+    def half_rows(c, first=0, count=HALF):
+        return pl.ds(pl.multiple_of(c * HALF + first, 64), count)
+
+    FAR_NEAR = ((0, core, jnp.where(core == 0, left, right)), (1, 1 - core, mate))
     swaps = []
-    for c in range(2):
-        pair = []
-        for n, d in enumerate((1, 3)):
-            part = frame.at[quarter, c * HALF : (c + 1) * HALF]
-            pair.append(post(part, part, xs.at[c, n], xr.at[c, n], s, x_peer(d)))
-        swaps.append(pair)
+    for k, c, _ in FAR_NEAR:
+        part = frame.at[quarter, half_rows(c)]
+        swaps.append(
+            [post(part, part, xs.at[k, n], xr.at[k, n], s, x_peer(d)) for n, d in enumerate((1, 3))]
+        )
     settle(1, kept)
 
     def share(tp, first):
@@ -264,22 +267,38 @@
 
     wo_share = share(z_peer, 13)
 
+    def group_peer(k):
+        return lax.rem(x_peer(k % NX) + k // NX * NX, TP)
+
+    w2_first = {}
+
+    def give_w2(steps):
+        for k in steps:
+            peer = group_peer(k)
+            cols = pl.ds(pl.multiple_of(peer * LW, LW), LW)
+            w2_first[k] = post(
+                w2.at[pl.ds(pl.multiple_of(core * 64, 64), 64), cols],
+                w2c.at[pl.ds(pl.multiple_of(t * LW + core * 64, 64), 64)],
+                w2s.at[k - 1], w2r.at[k - 1], s, peer,
+            )
+
+    give_w2(range(NX, TP))
+
     for cp in ld_qkv:
         cp.wait()
     halos = []
-    for c in range(2):
-        for cp in swaps[c]:
+    normed = []
+    for k, c, peer in FAR_NEAR:
+        for cp in swaps[k]:
             land(cp)
-        rows = slice(c * HALF, (c + 1) * HALF)
-        z1 = layer_norm([frame[q, rows, :].astype(F32) for q in range(4)], gain1)
-        kvx[WMAX + c * HALF : WMAX + (c + 1) * HALF, :] = dot(z1, wkv[...]).astype(BF16)
-        src = kvx.at[WMAX + c * HALF : WMAX + (c + 1) * HALF]
-        if c == 0:
-            cp = post(src, kvx.at[WMAX + ROWS : 2 * WMAX + ROWS], hs.at[0], hr.at[0], left, t)
-        else:
-            cp = post(src, kvx.at[0:WMAX], hs.at[1], hr.at[1], right, t)
-        halos.append(cp)
-        qv[rows, :] = dot(z1, wq[...]).astype(BF16)
+        z1 = layer_norm([frame[q, half_rows(c), :].astype(F32) for q in range(4)], gain1)
+        normed.append(z1)
+        here = half_rows(c, WMAX)
+        kvx[here, :] = dot(z1, wkv[...]).astype(BF16)
+        there = half_rows(3 * (1 - c))
+        halos.append(post(kvx.at[here], kvx.at[there], hs.at[k], hr.at[k], peer, t))
+    for k, c, _ in FAR_NEAR:
+        qv[half_rows(c), :] = dot(normed[k], wq[...]).astype(BF16)
 
     for cp in wo_share:
         land(cp)
@@ -331,7 +350,7 @@
         return jnp.concatenate([buf[k, rows, :] for k in range(TP)], axis=1)
 
     EDGES = (slice(192, 256), slice(0, 64))
-    PLACES = (slice(0, HALF), slice(HALF, 192))
+    PLACES = (slice(0, HALF), slice(HALF, ROWS))
     BLOCKS = (slice(0, HALF), slice(HALF, ROWS))
 
     def natural(ref_rows, c):
@@ -342,8 +361,8 @@
     scale = 1.0 / math.sqrt(LW)
 
     def masked_scores(c, first, count):
-        rows = slice(c * HALF, (c + 1) * HALF)
-        scores = dot_nt(qv[rows, :], kvx[first : first + count, 0:LW]) * scale
+        rows = half_rows(c)
+        scores = dot_nt(qv[rows, :], kvx[pl.ds(first, count), 0:LW]) * scale
         kpos = s * ROWS + first - WMAX + iota((HALF, count), 1)
         low = jnp.concatenate([lo_ref[rows, :]] * (count // LW), axis=1)
         high = jnp.concatenate([hi_ref[rows, :]] * (count // LW), axis=1)
@@ -356,29 +375,26 @@
         total = jnp.sum(weights, axis=1, keepdims=True)
         return peak, total, dot(weights.astype(BF16), kvx[WMAX : WMAX + ROWS, LW : 2 * LW])
 
-    own_part = {c: attend_own(c) for c in (1, 0)}
-    for c in (1, 0):
-        first = 0 if c == 0 else WMAX + ROWS
-        land(halos[1 - c])
+    own_part = [attend_own(c) for _, c, _ in FAR_NEAR]
+    for k in (1, 0):
+        c = FAR_NEAR[k][1]
+        first = pl.multiple_of(c * (WMAX + ROWS), HALF)
+        land(halos[k])
         scores = masked_scores(c, first, WMAX)
-        own_peak, own_total, own_sum = own_part[c]
+        own_peak, own_total, own_sum = own_part[k]
         peak = jnp.maximum(own_peak, jnp.max(scores, axis=1, keepdims=True))
         weights = jnp.exp(scores - peak)
         fade = jnp.exp(own_peak - peak)
         total = own_total * fade + jnp.sum(weights, axis=1, keepdims=True)
-        mixed = own_sum * fade + dot(weights.astype(BF16), kvx[first : first + WMAX, LW : 2 * LW])
+        mixed = own_sum * fade + dot(weights.astype(BF16), kvx[pl.ds(first, WMAX), LW : 2 * LW])
         mixed = (mixed / total).astype(BF16)
-        if c == 1:
-            ctx[t, 0:64, :] = mixed[64:128]
-            ctx[t, 192:256, :] = mixed[0:64]
-        else:
-            ctx[t, 64:192, :] = mixed
+        ctx[t, half_rows(c, 64, 64), :] = mixed[0:64]
+        ctx[t, half_rows(1 - c, 0, 64), :] = mixed[64:128]
     sent1 = {}
     for c in (0, 1):
         sent1[c] = send_group(ctx, PLACES[c], c1s.at[c], c1r.at[c], [z_peer], 0)
     for c in (0, 1):
         sent1[c] += send_group(ctx, PLACES[c], c1s.at[c], c1r.at[c], x_peers, 1)
-    straight = send_direct(ctx, slice(192, 256), c1s.at[2], c1r.at[2])
 
     z_opposite = lax.rem(x_peer(2) + NX, TP)
     land(wo_opposite)
@@ -390,18 +406,7 @@
     for c in (0, 1):
         pass_on(ctx, PLACES[c], c1s.at[c], c1r.at[c], sent1[c])
 
-    w2_first = []
-    for k in (4, 5, 3, 6, 2, 7, 1):
-        peer = lax.rem(t + k, TP)
-        w2_first.append(
-            post(
-                w2.at[
-                    pl.ds(pl.multiple_of(core * 64, 64), 64), pl.ds(pl.multiple_of(peer * LW, LW), LW)
-                ],
-                w2c.at[pl.ds(pl.multiple_of(t * LW + core * 64, 64), 64)],
-                w2s.at[k - 1], w2r.at[k - 1], s, peer,
-            )
-        )
+    give_w2(range(1, NX))
 
     for cp in wo_share_opposite:
         land(cp)
@@ -426,7 +431,7 @@
 
     edges = []
     for c in (0, 1):
-        attn = dot(whole(ctx, BLOCKS[c], sent1[c] + straight * c), wof[...])
+        attn = dot(whole(ctx, BLOCKS[c], sent1[c]), wof[...])
         resid = [
             (
                 natural(lambda rows: frame[q, rows, :], c).astype(F32)
@@ -475,9 +480,10 @@
     last = send_direct(act, slice(224, 256), c2s.at[3], c2r.at[3])
 
     w2_swap = []
-    for n, k in enumerate((4, 5, 3, 6, 2, 7, 1)):
-        land(w2_first[n])
-        part = w2c.at[pl.ds(pl.multiple_of(lax.rem(t + TP - k, TP) * LW + core * 64, 64), 64)]
+    for k in (4, 5, 6, 7, 1, 2, 3):
+        land(w2_first[k])
+        source = group_peer(k // NX * NX + (NX - k) % NX)
+        part = w2c.at[pl.ds(pl.multiple_of(source * LW + core * 64, 64), 64)]
         w2_swap.append(post(part, part, w2s.at[6 + k], w2r.at[6 + k], mate, t))
     for n, (begin, stop) in enumerate(PIECES):
         pass_on(act, slice(begin, stop), c2s.at[n], c2r.at[n], sent2[n])

time: 58.9 us -> 58.1 us (0.986)
  the two profiles are of different devices: /device:TPU:32 before, /device:TPU:1 now
where the time goes in v4:
time: 58.1 us; the launch traced here: 58 us
  Pallas kernels  56.5 us (97%)
  local copies, waits for them, and re-layouts  1.47 us (3%)
    pallas_call x1, Pallas kernels, local(): pl.pallas_call(block_kernel, out_shape=jax.ShapeDtypeStruct((ROWS, LW), B...  56.5 us
    unnamed x1, local copies, waits for them, and re-layouts  1.47 us

profile of v4, /device:TPU:1, one launch (start us, length us, event | category | flops | bytes accessed | tf_op | source)
XLA Modules:
  0.0 58.0 jit_solution(5418655251555347705)
XLA Ops:
  0.0 56.5 %encoder_block.1 = bf16[256,128]{1,0:T(8,128)(2,1)} custom-call(bf16[256,1024]{1,0:T(8,128)(2,1)} %frames.1, s32[64,64]{1,0:T(8,128)} %smap_hbm.1, s32[8]{0:T(128)} %lens_hbm.1, s32[8]{0:T(128)} %wins_hbm.1, f32[1,1024]{1,0:T(1,128)} %bitcast.4, bf16[3,1024,128]{2,1,0:T(8,128)(2,1)} %wqkv.1, bf16[128,1024]{1,0:T(8,128)(2,1)} %wo.1, f32[1,1024]{1,0:T(1,128)} %bitcast.5, ...), custom_call_target="tpu_custom_call" | custom-call | tf_op jit(solution)/shard_map/encoder_block/pallas_call | solution.py:518
  56.5 1.5 %copy.15 = bf16[256,128]{1,0:T(8,128)(2,1)} copy(bf16[256,128]{1,0:T(8,128)(2,1)} %encoder_block.1) | data formatting | bytes 131072

commit v5 on v4

--- a/solution.py
+++ b/solution.py
@@ -98,11 +98,12 @@
         cp.wait_recv()
         got.append(id(cp))
 
-    def drain():
-        for cp in flight:
-            if id(cp) not in got:
-                cp.wait_recv()
+    left_over = [0]
+
+    def flush(count):
+        for cp in flight[left_over[0] : count]:
             cp.wait_send()
+        left_over[0] = count
 
     parity = lax.rem(x, 2)
     quarter = 2 * parity + x // 2
@@ -390,6 +391,7 @@
         mixed = (mixed / total).astype(BF16)
         ctx[t, half_rows(c, 64, 64), :] = mixed[0:64]
         ctx[t, half_rows(1 - c, 0, 64), :] = mixed[64:128]
+    posted = len(flight)
     sent1 = {}
     for c in (0, 1):
         sent1[c] = send_group(ctx, PLACES[c], c1s.at[c], c1r.at[c], [z_peer], 0)
@@ -399,6 +401,9 @@
     z_opposite = lax.rem(x_peer(2) + NX, TP)
     land(wo_opposite)
     wo_share_opposite = share(z_opposite, 20)
+    for cp in deals:
+        cp.wait_send()
+    flush(posted)
 
     for n, d in enumerate((1, 3)):
         land(wo_next[n])
@@ -463,6 +468,7 @@
     for cp in ld_conv:
         cp.wait()
     PIECES = ((0, 80), (80, 160), (160, 224))
+    posted = len(flight)
     sent2 = []
     for n, (begin, stop) in enumerate(PIECES):
         act[t, begin:stop, :] = conv_act(EDGE + begin, stop - begin)
@@ -478,6 +484,7 @@
     act[t, 224:240, :] = conv_act(ROWS - EDGE, EDGE)
     act[t, 240:256, :] = conv_act(0, EDGE)
     last = send_direct(act, slice(224, 256), c2s.at[3], c2r.at[3])
+    flush(posted)
 
     w2_swap = []
     for k in (4, 5, 6, 7, 1, 2, 3):
@@ -485,11 +492,13 @@
         source = group_peer(k // NX * NX + (NX - k) % NX)
         part = w2c.at[pl.ds(pl.multiple_of(source * LW + core * 64, 64), 64)]
         w2_swap.append(post(part, part, w2s.at[6 + k], w2r.at[6 + k], mate, t))
+    posted = len(flight)
     for n, (begin, stop) in enumerate(PIECES):
         pass_on(act, slice(begin, stop), c2s.at[n], c2r.at[n], sent2[n])
     ld_w2.wait()
     for cp in w2_swap:
         land(cp)
+    flush(posted)
 
     def finish(first, count, begin, sent):
         summed = dot(whole(act, slice(begin, begin + count), sent), w2c[...])
@@ -502,11 +511,8 @@
     finish(0, EDGE, 240, last)
     cp = pltpu.make_async_copy(outv, out, out_sem)
     cp.start()
+    flush(len(flight))
     cp.wait()
-
-    for cp in deals:
-        cp.wait_send()
-    drain()
 
 
 def local(

time: 58.1 us -> 58 us (level)
  no operation moved by 1% of the time
where the time goes in v5:
time: 58 us; the launch traced here: 57.8 us
  Pallas kernels  56.3 us (97%)
  local copies, waits for them, and re-layouts  1.47 us (3%)
    pallas_call x1, Pallas kernels, local(): pl.pallas_call(block_kernel, out_shape=jax.ShapeDtypeStruct((ROWS, LW), B...  56.3 us
    unnamed x1, local copies, waits for them, and re-layouts  1.47 us

profile of v5, /device:TPU:1, one launch (start us, length us, event | category | flops | bytes accessed | tf_op | source)
XLA Modules:
  0.0 57.8 jit_solution(14916557207868470063)
XLA Ops:
  0.0 56.3 %encoder_block.1 = bf16[256,128]{1,0:T(8,128)(2,1)} custom-call(bf16[256,1024]{1,0:T(8,128)(2,1)} %frames.1, s32[64,64]{1,0:T(8,128)} %smap_hbm.1, s32[8]{0:T(128)} %lens_hbm.1, s32[8]{0:T(128)} %wins_hbm.1, f32[1,1024]{1,0:T(1,128)} %bitcast.4, bf16[3,1024,128]{2,1,0:T(8,128)(2,1)} %wqkv.1, bf16[128,1024]{1,0:T(8,128)(2,1)} %wo.1, f32[1,1024]{1,0:T(1,128)} %bitcast.5, ...), custom_call_target="tpu_custom_call" | custom-call | tf_op jit(solution)/shard_map/encoder_block/pallas_call | solution.py:524
  56.3 1.5 %copy.15 = bf16[256,128]{1,0:T(8,128)(2,1)} copy(bf16[256,128]{1,0:T(8,128)(2,1)} %encoder_block.1) | data formatting | bytes 131072

commit v6 on v5

--- a/solution.py
+++ b/solution.py
@@ -405,13 +405,11 @@
         cp.wait_send()
     flush(posted)
 
+    pass_on(ctx, PLACES[0], c1s.at[0], c1r.at[0], sent1[0])
     for n, d in enumerate((1, 3)):
         land(wo_next[n])
         give_wo(lax.rem(x_peer(NX - d) + NX, TP))
-    for c in (0, 1):
-        pass_on(ctx, PLACES[c], c1s.at[c], c1r.at[c], sent1[c])
-
-    give_w2(range(1, NX))
+    pass_on(ctx, PLACES[1], c1s.at[1], c1r.at[1], sent1[1])
 
     for cp in wo_share_opposite:
         land(cp)
@@ -436,7 +434,10 @@
 
     edges = []
     for c in (0, 1):
-        attn = dot(whole(ctx, BLOCKS[c], sent1[c]), wof[...])
+        gathered = whole(ctx, BLOCKS[c], sent1[c])
+        if c == 1:
+            give_w2(range(1, NX))
+        attn = dot(gathered, wof[...])
         resid = [
             (
                 natural(lambda rows: frame[q, rows, :], c).astype(F32)

time: 58 us -> 58 us (level)
  no operation moved by 1% of the time
where the time goes in v6:
time: 58 us; the launch traced here: 57.8 us
  Pallas kernels  56.3 us (97%)
  local copies, waits for them, and re-layouts  1.47 us (3%)
    pallas_call x1, Pallas kernels, local(): pl.pallas_call(block_kernel, out_shape=jax.ShapeDtypeStruct((ROWS, LW), B...  56.3 us
    unnamed x1, local copies, waits for them, and re-layouts  1.47 us

profile of v6, /device:TPU:1, one launch (start us, length us, event | category | flops | bytes accessed | tf_op | source)
XLA Modules:
  0.0 57.8 jit_solution(8215419503497225947)
XLA Ops:
  0.0 56.3 %encoder_block.1 = bf16[256,128]{1,0:T(8,128)(2,1)} custom-call(bf16[256,1024]{1,0:T(8,128)(2,1)} %frames.1, s32[64,64]{1,0:T(8,128)} %smap_hbm.1, s32[8]{0:T(128)} %lens_hbm.1, s32[8]{0:T(128)} %wins_hbm.1, f32[1,1024]{1,0:T(1,128)} %bitcast.4, bf16[3,1024,128]{2,1,0:T(8,128)(2,1)} %wqkv.1, bf16[128,1024]{1,0:T(8,128)(2,1)} %wo.1, f32[1,1024]{1,0:T(1,128)} %bitcast.5, ...), custom_call_target="tpu_custom_call" | custom-call | tf_op jit(solution)/shard_map/encoder_block/pallas_call | solution.py:525
  56.3 1.5 %copy.15 = bf16[256,128]{1,0:T(8,128)(2,1)} copy(bf16[256,128]{1,0:T(8,128)(2,1)} %encoder_block.1) | data formatting | bytes 131072
